TPU v7x, 512 devices: a whole 4x8x8 slice. The times are simulated.
512 devices in a mesh: ctx: 16 (over y, core), tp: 32 (over x, z).
Axes of the slice: x: 4, y: 8, z: 8, core: 2. Of those that a mesh axis runs over, the one named last changes fastest.
Arguments:
- queries: bfloat16 [16384, 8192], P('ctx', 'tp'), may hold values from -30 to 30
- keys: bfloat16 [16384, 1024], P('ctx', 'tp'), may hold values from -30 to 30
- values: bfloat16 [16384, 1024], P('ctx', 'tp'), may hold values from -6 to 6
- grad_out: bfloat16 [16384, 8192], P('ctx', 'tp'), may hold values from -24 to 24
- doc_lengths: int32 [32], replicated, may hold values from 1 to 1024, 16384 in all
Outputs:
- attention_out: bfloat16 [16384, 8192], P('ctx', 'tp')
- grad_queries: bfloat16 [16384, 8192], P('ctx', 'tp')
- grad_keys: bfloat16 [16384, 1024], P('ctx', 'tp')
- grad_values: bfloat16 [16384, 1024], P('ctx', 'tp')
All inputs are finite; a program needn't handle non-finite values.
Results may differ from a plain program's by a relative error of at most 0.025.
Values may be sent and summed in bfloat16 or wider, within the bound.
A program may use at most 128 MiB of HBM per device.

v0:
```python
import math

import jax
import jax.numpy as jnp
from jax import lax
from jax.sharding import PartitionSpec as P

HD = 128
DOCMAX = 1024


NEG_FILL = -1e30


def swapped(value, axis, distance):
    mask = 2**distance
    pairs = [(source, source ^ mask) for source in range(lax.axis_size(axis))]
    return lax.ppermute(value, axis, pairs)


def passed_along(value, axis, by):
    size = lax.axis_size(axis)
    pairs = [(i, i + by) for i in range(size) if 0 <= i + by < size]
    return lax.ppermute(value, axis, pairs)


def segment_ids(positions, doc_ends):
    return jnp.sum((doc_ends[None, :] <= positions[:, None]).astype(jnp.int32), axis=1)


def allowed_pairs(query_pos, query_seg, key_pos, key_seg):
    same_doc = query_seg[:, None] == key_seg[None, :]
    causal = key_pos[None, :] <= query_pos[:, None]
    return same_doc & causal & (key_pos[None, :] >= 0)


def halve_columns(stacked, tp_place, levels, partner):
    for bit_level in reversed(range(levels)):
        half_width = stacked.shape[2] // 2
        place_bit = tp_place >> bit_level & 1
        kept_half = lax.dynamic_slice_in_dim(stacked, place_bit * half_width, half_width, 2)
        sent_half = lax.dynamic_slice_in_dim(stacked, (1 - place_bit) * half_width, half_width, 2)
        stacked = kept_half + partner(sent_half, bit_level)
    return stacked


def on_device(queries, keys, values, grad_out, doc_lengths):
    tokens = queries.shape[0]
    heads_here = queries.shape[1] // HD
    columns = keys.shape[1]
    levels = (HD // columns).bit_length() - 1
    block_len = min(512, tokens)
    tile_count = (DOCMAX + block_len) // block_len
    score_scale = 1.0 / math.sqrt(HD)
    doc_ends = jnp.cumsum(doc_lengths)
    tp_place = lax.axis_index("tp")
    start_pos = lax.axis_index("ctx") * tokens
    window_pos = start_pos - tokens + jnp.arange(2 * tokens, dtype=jnp.int32)
    window_seg = segment_ids(window_pos, doc_ends)
    kv_pair = jnp.stack([keys, values])
    for bit_level in range(levels):
        partner_cols = swapped(kv_pair, "tp", bit_level)
        place_bit = tp_place >> bit_level & 1
        kv_pair = jnp.where(
            place_bit == 0,
            jnp.concatenate([kv_pair, partner_cols], 2),
            jnp.concatenate([partner_cols, kv_pair], 2),
        )
    previous = passed_along(kv_pair, "ctx", 1)
    window = jnp.concatenate([previous, kv_pair], 1)
    key_window = window[0]
    value_window = window[1]
    query_heads = queries.reshape(tokens, heads_here, HD)
    grad_heads = grad_out.reshape(tokens, heads_here, HD)
    out_blocks = []
    query_grads = []
    kv_grads = jnp.zeros((2, 2 * tokens, HD), jnp.float32)
    for row_start in range(0, tokens, block_len):
        query_block = query_heads[row_start : row_start + block_len]
        grad_block = grad_heads[row_start : row_start + block_len]
        query_pos = window_pos[tokens + row_start : tokens + row_start + block_len]
        query_seg = window_seg[tokens + row_start : tokens + row_start + block_len]
        tile_starts = [
            tokens + row_start - DOCMAX + number * block_len for number in range(tile_count)
        ]
        tile_masks = [
            allowed_pairs(
                query_pos,
                query_seg,
                window_pos[begin : begin + block_len],
                window_seg[begin : begin + block_len],
            )
            for begin in tile_starts
        ]
        running_max = jnp.full((heads_here, block_len), NEG_FILL, jnp.float32)
        running_sum = jnp.zeros((heads_here, block_len), jnp.float32)
        tile_scores_list = []
        for start_at, tile_mask in zip(tile_starts, tile_masks):

            def gather_stats(
                start_at=start_at,
                tile_mask=tile_mask,
                running_max=running_max,
                running_sum=running_sum,
                query_block=query_block,
            ):
                raw_scores = (
                    jnp.einsum(
                        "qhd,kd->hqk",
                        query_block,
                        key_window[start_at : start_at + block_len],
                        preferred_element_type=jnp.float32,
                    )
                    * score_scale
                )
                tile_scores = jnp.where(tile_mask[None], raw_scores, NEG_FILL)
                higher = jnp.maximum(running_max, jnp.max(tile_scores, axis=2))
                kept_terms = jnp.where(
                    tile_mask[None], jnp.exp(tile_scores - higher[:, :, None]), 0.0
                )
                return (
                    higher,
                    running_sum * jnp.exp(running_max - higher) + jnp.sum(kept_terms, axis=2),
                    tile_scores,
                )

            running_max, running_sum, tile_scores = gather_stats()
            tile_scores_list.append(tile_scores)
        log_total = running_max + jnp.log(running_sum)
        acc_out = jnp.zeros((block_len, heads_here, HD), jnp.float32)
        prob_list = []
        for start_at, tile_mask, tile_scores in zip(tile_starts, tile_masks, tile_scores_list):

            def add_values(
                start_at=start_at, tile_mask=tile_mask, tile_scores=tile_scores, acc_out=acc_out
            ):
                prob_high = jnp.where(
                    tile_mask[None], jnp.exp(tile_scores - log_total[:, :, None]), 0.0
                )
                prob_low = prob_high.astype(jnp.bfloat16)
                added = acc_out + jnp.einsum(
                    "hqk,kd->qhd",
                    prob_low,
                    value_window[start_at : start_at + block_len],
                    preferred_element_type=jnp.float32,
                )
                return (added, prob_high, prob_low)

            acc_out, prob_high, prob_low = add_values()
            prob_list.append((prob_high, prob_low))
        out_block = acc_out.astype(jnp.bfloat16)
        row_delta = jnp.sum(
            grad_block.astype(jnp.float32) * out_block.astype(jnp.float32), axis=2
        ).T
        out_blocks.append(out_block)
        acc_query = jnp.zeros((block_len, heads_here, HD), jnp.float32)
        for start_at, tile_mask, probs in zip(tile_starts, tile_masks, prob_list):

            def add_grads(
                start_at=start_at,
                probs=probs,
                acc_query=acc_query,
                kv_grads=kv_grads,
                query_block=query_block,
                grad_block=grad_block,
                row_delta=row_delta,
            ):
                prob_high, prob_low = probs
                key_tile = key_window[start_at : start_at + block_len]
                value_tile = value_window[start_at : start_at + block_len]
                grad_prob = jnp.einsum(
                    "qhd,kd->hqk", grad_block, value_tile, preferred_element_type=jnp.float32
                )
                dscore = (prob_high * (grad_prob - row_delta[:, :, None]) * score_scale).astype(
                    jnp.bfloat16
                )
                next_query = acc_query + jnp.einsum(
                    "hqk,kd->qhd", dscore, key_tile, preferred_element_type=jnp.float32
                )
                key_term = jnp.einsum(
                    "hqk,qhd->kd", dscore, query_block, preferred_element_type=jnp.float32
                )
                value_term = jnp.einsum(
                    "hqk,qhd->kd", prob_low, grad_block, preferred_element_type=jnp.float32
                )
                return (
                    next_query,
                    kv_grads.at[:, start_at : start_at + block_len].add(
                        jnp.stack([key_term, value_term])
                    ),
                )

            acc_query, kv_grads = add_grads()
        query_grads.append(acc_query.astype(jnp.bfloat16))
    attention_out = jnp.concatenate(out_blocks, 0).reshape(tokens, heads_here * HD)
    grad_queries = jnp.concatenate(query_grads, 0).reshape(tokens, heads_here * HD)
    earlier = kv_grads[:, :tokens]
    own_terms = kv_grads[:, tokens:]
    returned = passed_along(earlier.astype(jnp.bfloat16), "ctx", -1).astype(earlier.dtype)

    def grad_partner(sent_half, bit_level):
        return swapped(sent_half, "tp", bit_level)

    summed = halve_columns(own_terms + returned, tp_place, levels, grad_partner)
    return (
        attention_out,
        grad_queries,
        summed[0].astype(jnp.bfloat16),
        summed[1].astype(jnp.bfloat16),
    )


def solution(mesh):
    in_specs = (P("ctx", "tp"), P("ctx", "tp"), P("ctx", "tp"), P("ctx", "tp"), P())
    out_specs = (P("ctx", "tp"), P("ctx", "tp"), P("ctx", "tp"), P("ctx", "tp"))
    return jax.shard_map(
        on_device, mesh=mesh, in_specs=in_specs, out_specs=out_specs, check_vma=False
    )
```

profile of v0, /device:TPU:46, one launch (start us, length us, event | category | flops | bytes accessed | tf_op | source)
XLA Modules:
  0.0 128.4 jit_solution(10132870881315995588)
XLA Ops:
  0.6 0.9 pad_maximum_fusion.2
  1.9 4.3 %collective-permute-start = (bf16[2,1024,32]{2,1,0:T(8,128)(2,1)S(1)}, bf16[2,1024,32]{2,1,0:T(8,128)(2,1)S(1)}, u32[]{:S(2)}, u32[]{:S(2)}) collective-permute-start(bf16[2,1024,32]{2,1,0:T(8,128)(2,1)S(1)} %copy.180), channel_id=1, source_target_pairs={{0,1},{1,0},{2,3},{3,2},{4,5},{5,4},{6,7},{7,6},{8,9},{9,8},{10,11... | collective-permute-start | bytes 393224 | tf_op jit(solution)/shard_map/ppermute | solution.py:18
  6.2 0.7 copy.182
  7.2 1.1 fusion.79
  9.0 9.1 %collective-permute-done = bf16[2,1024,32]{2,1,0:T(8,128)(2,1)S(1)} collective-permute-done((bf16[2,1024,32]{2,1,0:T(8,128)(2,1)S(1)}, bf16[2,1024,32]{2,1,0:T(8,128)(2,1)S(1)}, u32[]{:S(2)}, u32[]{:S(2)}) %collective-permute-start) | collective-permute-done | bytes 131104 | tf_op jit(solution)/shard_map/ppermute | solution.py:18
  18.6 6.1 %collective-permute-start.1 = (bf16[2,1024,64]{2,1,0:T(8,128)(2,1)S(1)}, bf16[2,1024,64]{2,1,0:T(8,128)(2,1)S(1)}, u32[]{:S(2)}, u32[]{:S(2)}) collective-permute-start(bf16[2,1024,64]{2,1,0:T(8,128)(2,1)S(1)} %maximum_select_fusion), channel_id=1, source_target_pairs={{0,2},{1,3},{2,0},{3,1},{4,6},{5,7},{6,4},{7,5},{8,10},{9,11},{10,... | collective-permute-start | bytes 786440 | tf_op jit(solution)/shard_map/ppermute | solution.py:18
  24.7 1.9 %and_and_fusion.4 = (pred[512,512]{0,1:T(8,128)(4,1)S(1)}, pred[512,512]{0,1:T(8,128)(4,1)S(1)}, pred[512,512]{0,1:T(8,128)(4,1)S(1)}, pred[512,512]{0,1:T(8,128...) fusion(s32[512]{0:T(512)S(1)} %get-tuple-element.113, s32[512]{0:T(512)S(1)} %get-tuple-element.109, ...), kind=kLoop, calls=%fused_computation.84 | loop fusion | flops 6291456 | bytes 1591296 | tf_op jit(solution)/shard_map/and | solution.py:34
  26.6 20.7 %collective-permute-done.1 = bf16[2,1024,64]{2,1,0:T(8,128)(2,1)S(1)} collective-permute-done((bf16[2,1024,64]{2,1,0:T(8,128)(2,1)S(1)}, bf16[2,1024,64]{2,1,0:T(8,128)(2,1)S(1)}, u32[]{:S(2)}, u32[]{:S(2)}) %collective-permute-start.1) | collective-permute-done | bytes 262176 | tf_op jit(solution)/shard_map/ppermute | solution.py:18
  47.9 2.1 %collective-permute-start.2 = (bf16[2,1024,128]{2,1,0:T(8,128)(2,1)S(1)}, bf16[2,1024,128]{2,1,0:T(8,128)(2,1)S(1)}, u32[]{:S(2)}, u32[]{:S(2)}) collective-permute-start(bf16[2,1024,128]{2,1,0:T(8,128)(2,1)S(1)} %maximum_select_fusion.1), channel_id=1, source_target_pairs={{0,32},{32,64},{64,96},{96,128},{128,160},{160,192},{192,224},{224... | collective-permute-start | bytes 1572872 | tf_op jit(solution)/shard_map/ppermute | solution.py:24
  51.7 6.8 %collective-permute-done.2 = bf16[2,1024,128]{2,1,0:T(8,128)(2,1)S(1)} collective-permute-done((bf16[2,1024,128]{2,1,0:T(8,128)(2,1)S(1)}, bf16[2,1024,128]{2,1,0:T(8,128)(2,1)S(1)}, u32[]{:S(2)}, u32[]{:S(2)}) %collective-permute-start.2) | collective-permute-done | bytes 524320 | tf_op jit(solution)/shard_map/ppermute | solution.py:24
  60.1 0.8 select_reduce_fusion.4
  60.9 0.8 select_reduce_fusion.2
  64.4 0.8 select_reduce_fusion
  66.6 0.6 convolution_bitcast_fusion.4
  67.2 0.6 convolution_bitcast_fusion.2
  68.5 0.7 multiply_reduce_fusion
  69.2 0.8 fusion.5
  70.0 1.0 fusion.2
  71.7 0.7 multiply_reduce_fusion.1
  72.3 0.8 fusion.11
  73.9 0.8 fusion.17
  75.2 0.8 fusion.14
  76.5 0.8 fusion.8
  79.8 1.9 %collective-permute-start.3 = (bf16[2,1024,128]{1,2,0:T(8,128)(2,1)S(1)}, bf16[2,1024,128]{1,2,0:T(8,128)(2,1)S(1)}, u32[]{:S(2)}, u32[]{:S(2)}) collective-permute-start(bf16[2,1024,128]{1,2,0:T(8,128)(2,1)S(1)} %slice.408), channel_id=1, source_target_pairs={{32,0},{64,32},{96,64},{128,96},{160,128},{192,160},{224,192},{256... | collective-permute-start | bytes 1572872 | tf_op jit(solution)/shard_map/ppermute | solution.py:24
  82.3 6.0 %collective-permute-done.3 = bf16[2,1024,128]{1,2,0:T(8,128)(2,1)S(1)} collective-permute-done((bf16[2,1024,128]{1,2,0:T(8,128)(2,1)S(1)}, bf16[2,1024,128]{1,2,0:T(8,128)(2,1)S(1)}, u32[]{:S(2)}, u32[]{:S(2)}) %collective-permute-start.3) | collective-permute-done | bytes 524320 | tf_op jit(solution)/shard_map/ppermute | solution.py:24
  88.6 1.9 %collective-permute-start.4 = (f32[2,1024,64]{1,2,0:T(8,128)S(1)}, f32[2,1024,64]{1,2,0:T(8,128)S(1)}, u32[]{:S(2)}, u32[]{:S(2)}) collective-permute-start(f32[2,1024,64]{1,2,0:T(8,128)S(1)} %constant_dynamic-slice_fusion.1), channel_id=1, source_target_pairs={{0,2},{1,3},{2,0},{3,1},{4,6},{5,7},{6,4},{7,5},{8,10},{9,11},{10,... | collective-permute-start | bytes 1572872 | tf_op jit(solution)/shard_map/ppermute | solution.py:18
  91.2 26.2 %collective-permute-done.4 = f32[2,1024,64]{1,2,0:T(8,128)S(1)} collective-permute-done((f32[2,1024,64]{1,2,0:T(8,128)S(1)}, f32[2,1024,64]{1,2,0:T(8,128)S(1)}, u32[]{:S(2)}, u32[]{:S(2)}) %collective-permute-start.4) | collective-permute-done | bytes 524320 | tf_op jit(solution)/shard_map/ppermute | solution.py:18
  117.5 1.9 %collective-permute-start.5 = (f32[2,1024,32]{1,2,0:T(8,128)S(1)}, f32[2,1024,32]{1,2,0:T(8,128)S(1)}, u32[]{:S(2)}, u32[]{:S(2)}) collective-permute-start(f32[2,1024,32]{1,2,0:T(8,128)S(1)} %constant_dynamic-slice_fusion), channel_id=1, source_target_pairs={{0,1},{1,0},{2,3},{3,2},{4,5},{5,4},{6,7},{7,6},{8,9},{9,8},{10,11... | collective-permute-start | bytes 786440 | tf_op jit(solution)/shard_map/ppermute | solution.py:18
  119.8 1.0 copy.236
  120.9 1.0 copy.235
  121.9 5.8 %collective-permute-done.5 = f32[2,1024,32]{1,2,0:T(8,128)S(1)} collective-permute-done((f32[2,1024,32]{1,2,0:T(8,128)S(1)}, f32[2,1024,32]{1,2,0:T(8,128)S(1)}, u32[]{:S(2)}, u32[]{:S(2)}) %collective-permute-start.5) | collective-permute-done | bytes 262176 | tf_op jit(solution)/shard_map/ppermute | solution.py:18
  127.7 0.7 slice_bitcast_fusion.32
  (61 shorter events, 16.9 us)
Async XLA Ops:
  0.6 8.0 %copy-start = (bf16[1024,256]{1,0:T(8,128)(2,1)S(1)}, bf16[1024,256]{1,0:T(8,128)(2,1)}, u32[]{:S(2)}) copy-start(bf16[1024,256]{1,0:T(8,128)(2,1)} %param.20) | copy-start | bytes 1572868
  1.9 16.2 %collective-permute-start = (bf16[2,1024,32]{2,1,0:T(8,128)(2,1)S(1)}, bf16[2,1024,32]{2,1,0:T(8,128)(2,1)S(1)}, u32[]{:S(2)}, u32[]{:S(2)}) collective-permute-start(bf16[2,1024,32]{2,1,0:T(8,128)(2,1)S(1)} %copy.180), channel_id=1, source_target_pairs={{0,1},{1,0},{2,3},{3,2},{4,5},{5,4},{6,7},{7,6},{8,9},{9,8},{10,11... | collective-permute-start | bytes 393224 | tf_op jit(solution)/shard_map/ppermute | solution.py:18
  18.6 28.7 %collective-permute-start.1 = (bf16[2,1024,64]{2,1,0:T(8,128)(2,1)S(1)}, bf16[2,1024,64]{2,1,0:T(8,128)(2,1)S(1)}, u32[]{:S(2)}, u32[]{:S(2)}) collective-permute-start(bf16[2,1024,64]{2,1,0:T(8,128)(2,1)S(1)} %maximum_select_fusion), channel_id=1, source_target_pairs={{0,2},{1,3},{2,0},{3,1},{4,6},{5,7},{6,4},{7,5},{8,10},{9,11},{10,... | collective-permute-start | bytes 786440 | tf_op jit(solution)/shard_map/ppermute | solution.py:18
  47.9 10.5 %collective-permute-start.2 = (bf16[2,1024,128]{2,1,0:T(8,128)(2,1)S(1)}, bf16[2,1024,128]{2,1,0:T(8,128)(2,1)S(1)}, u32[]{:S(2)}, u32[]{:S(2)}) collective-permute-start(bf16[2,1024,128]{2,1,0:T(8,128)(2,1)S(1)} %maximum_select_fusion.1), channel_id=1, source_target_pairs={{0,32},{32,64},{64,96},{96,128},{128,160},{160,192},{192,224},{224... | collective-permute-start | bytes 1572872 | tf_op jit(solution)/shard_map/ppermute | solution.py:24
  79.8 8.6 %collective-permute-start.3 = (bf16[2,1024,128]{1,2,0:T(8,128)(2,1)S(1)}, bf16[2,1024,128]{1,2,0:T(8,128)(2,1)S(1)}, u32[]{:S(2)}, u32[]{:S(2)}) collective-permute-start(bf16[2,1024,128]{1,2,0:T(8,128)(2,1)S(1)} %slice.408), channel_id=1, source_target_pairs={{32,0},{64,32},{96,64},{128,96},{160,128},{192,160},{224,192},{256... | collective-permute-start | bytes 1572872 | tf_op jit(solution)/shard_map/ppermute | solution.py:24
  88.6 28.8 %collective-permute-start.4 = (f32[2,1024,64]{1,2,0:T(8,128)S(1)}, f32[2,1024,64]{1,2,0:T(8,128)S(1)}, u32[]{:S(2)}, u32[]{:S(2)}) collective-permute-start(f32[2,1024,64]{1,2,0:T(8,128)S(1)} %constant_dynamic-slice_fusion.1), channel_id=1, source_target_pairs={{0,2},{1,3},{2,0},{3,1},{4,6},{5,7},{6,4},{7,5},{8,10},{9,11},{10,... | collective-permute-start | bytes 1572872 | tf_op jit(solution)/shard_map/ppermute | solution.py:18
  117.5 10.2 %collective-permute-start.5 = (f32[2,1024,32]{1,2,0:T(8,128)S(1)}, f32[2,1024,32]{1,2,0:T(8,128)S(1)}, u32[]{:S(2)}, u32[]{:S(2)}) collective-permute-start(f32[2,1024,32]{1,2,0:T(8,128)S(1)} %constant_dynamic-slice_fusion), channel_id=1, source_target_pairs={{0,1},{1,0},{2,3},{3,2},{4,5},{5,4},{6,7},{7,6},{8,9},{9,8},{10,11... | collective-permute-start | bytes 786440 | tf_op jit(solution)/shard_map/ppermute | solution.py:18
where the time goes:
time: 129 us; the launch traced here: 128 us
  waiting for transfers between devices  74.6 us (58%)
  matrix products  20.8 us (16%)
  starting transfers between devices  18.2 us (14%)
  other arithmetic  8.1 us (6%)
  local copies, waits for them, and re-layouts  5.5 us (4%)
    ppermute x4, waiting for transfers between devices, swapped(): return lax.ppermute(value, axis, pairs)  61.8 us
    ppermute x4, starting transfers between devices, swapped(): return lax.ppermute(value, axis, pairs)  14.2 us
    ppermute x2, waiting for transfers between devices, passed_along(): return lax.ppermute(value, axis, pairs)  12.8 us
    dot_general x6, matrix products, add_grads(): jnp.einsum('qhd,kd->hqk', grad_block, value_tile, preferred_element_type=...  5.08 us
    ppermute x2, starting transfers between devices, passed_along(): return lax.ppermute(value, axis, pairs)  4.02 us
    dot_general x6, matrix products, add_values(): jnp.einsum('hqk,kd->qhd', prob_low, value_window[start_at:start_at + bloc...  3.88 us
    dot_general x6, matrix products, add_grads(): jnp.einsum('hqk,qhd->kd', prob_low, grad_block, preferred_element_type=jn...  3.83 us
    dot_general x6, matrix products, gather_stats(): jnp.einsum('qhd,kd->hqk', query_block, key_window[start_at:start_at + blo...  3.25 us
  transfers between devices with their start and end apart: 6, of which 6 were waited for; matrix products, arithmetic and copies ran while one was open for 8% of the time, Pallas kernels for 0%

commit v1 on v0

v1 whole, which is shorter than its diff:
```python
import functools
import math

import jax
import jax.numpy as jnp
from jax import lax
from jax.experimental import pallas as pl
from jax.experimental.pallas import tpu as pltpu
from jax.sharding import PartitionSpec as P

HD = 128
BLK = 256
NEG_FILL = -1e30
MESH = pl.DeviceIdType.MESH


def dot(a, b):
    return jnp.dot(a, b, preferred_element_type=jnp.float32)


def kernel(
    n_ctx,
    tokens,
    share,
    doc_ref,
    q_hbm,
    kt_hbm,
    vt_hbm,
    do_hbm,
    out_hbm,
    dq_hbm,
    dkt_hbm,
    dvt_hbm,
    q_ref,
    do_ref,
    qt_ref,
    dot_ref,
    kv_ref,
    k_ref,
    v_ref,
    start_ref,
    s_ref,
    p_ref,
    out_ref,
    dq_ref,
    ret_send,
    ret_recv,
    total_ref,
    rs_send,
    rs_recv,
    fin_ref,
    load_sem,
    store_sem,
    g_send,
    g_recv,
    f_send,
    f_recv,
    b_send,
    b_recv,
    r_send,
    r_recv,
):
    scale = 1.0 / math.sqrt(HD)
    factor = scale * math.log2(math.e)
    ctx = lax.axis_index("ctx")
    tp = lax.axis_index("tp")
    place = lax.rem(tp, share)
    base = tp - place
    band = HD // share
    nxt = lax.rem(ctx + 1, n_ctx)
    prv = lax.rem(ctx + n_ctx - 1, n_ctx)
    span = tokens + BLK
    blocks = tokens // BLK
    own = pl.ds(tokens, tokens)
    before = pl.ds(0, tokens)
    kv_hbm = (kt_hbm, vt_hbm)

    def other(d):
        return lax.rem(place + d, share)

    def band_of(index):
        return pl.ds(pl.multiple_of(index * band, band), band)

    load_q = pltpu.make_async_copy(q_hbm, q_ref, load_sem.at[0])
    load_do = pltpu.make_async_copy(do_hbm, do_ref, load_sem.at[1])
    load_kv = [
        pltpu.make_async_copy(
            kv_hbm[i], kv_ref.at[i, band_of(place), own], load_sem.at[2 + i]
        )
        for i in range(2)
    ]
    for c in [load_q, load_do] + load_kv:
        c.start()

    barrier = pltpu.get_barrier_semaphore()
    for d in range(1, share):
        pl.semaphore_signal(
            barrier, inc=1, device_id=(ctx, base + other(d)), device_id_type=MESH
        )
    for c in (nxt, prv):
        pl.semaphore_signal(barrier, inc=1, device_id=(c, tp), device_id_type=MESH)
    pl.semaphore_wait(barrier, share + 1)

    def gather(i):
        copies = [
            pltpu.make_async_remote_copy(
                src_ref=kv_hbm[i],
                dst_ref=kv_ref.at[i, band_of(place), own],
                send_sem=g_send.at[i, d - 1],
                recv_sem=g_recv.at[i, d - 1],
                device_id=(ctx, base + other(d)),
                device_id_type=MESH,
            )
            for d in range(1, share)
        ]
        return copies

    def forward(i, d):
        which = lax.rem(place - d + share, share)
        src = kv_hbm[i] if d == 0 else kv_ref.at[i, band_of(which), own]
        return pltpu.make_async_remote_copy(
            src_ref=src,
            dst_ref=kv_ref.at[i, band_of(which), before],
            send_sem=f_send.at[i, d],
            recv_sem=f_recv.at[i, d],
            device_id=(nxt, tp),
            device_id_type=MESH,
        )

    gathers = [gather(i) for i in range(2)]
    forwards = [[forward(i, d) for d in range(share)] for i in range(2)]

    for c in gathers[0]:
        c.start()
    forwards[0][0].start()

    row_base = ctx * tokens
    window_base = row_base - tokens

    ends = []
    running = doc_ref[0]
    for k in range(1, doc_ref.shape[0]):
        ends.append(running)
        running = running + doc_ref[k]
    lane = lax.broadcasted_iota(jnp.int32, (128, 128), 1)
    sub = lax.broadcasted_iota(jnp.int32, (128, 128), 0)

    def find_start(chunk, carry):
        pos = sub + (row_base + chunk * 128)
        first = jnp.zeros((128, 128), jnp.int32)
        for e in ends:
            first = jnp.where(pos >= e, e, first)
        rows = pl.ds(pl.multiple_of(chunk * 128, 128), 128)
        start_ref[rows, :] = first - window_base - lane
        return carry

    lax.fori_loop(0, tokens // 128, find_start, 0)
    load_q.wait()
    qt_ref[...] = q_ref[...].T
    load_do.wait()
    dot_ref[...] = do_ref[...].T

    for d in range(1, share):
        gathers[0][d - 1].wait_recv()
        forwards[0][d].start()
    for c in gathers[1]:
        c.start()
    forwards[1][0].start()
    load_kv[0].wait()
    for d in range(share):
        forwards[0][d].wait_recv()

    lane32 = lax.broadcasted_iota(jnp.int32, (32, 128), 1)
    sub32 = lax.broadcasted_iota(jnp.int32, (32, 128), 0)

    def heads_of(ref, rows):
        return jnp.concatenate([ref[rows, 0:HD], ref[rows, HD : 2 * HD]], axis=0)

    def probabilities(b, carry):
        off = pl.multiple_of(b * BLK, BLK)
        rows = pl.ds(off, BLK)
        window = pl.ds(off, span)
        s_ref[...] = dot(heads_of(q_ref, rows), kv_ref[0, :, window])
        for r in range(0, 2 * BLK, 32):
            head, low = r // BLK, r % BLK
            these = pl.ds(off + low, 32)
            begin = start_ref[these, :] - off
            parts = []
            for j in range(span // 128):
                part = s_ref[r : r + 32, j * 128 : j * 128 + 128]
                ok = begin <= j * 128
                first = j * 128 - tokens
                if first + 127 > low:
                    ok = ok & (lane32 + first <= sub32 + low)
                parts.append(jnp.where(ok, part, NEG_FILL))
            scores = jnp.concatenate(parts, axis=1)
            top = jnp.max(scores, axis=1, keepdims=True)
            prob = jnp.exp2((scores - top) * factor)
            total = jnp.sum(prob, axis=1, keepdims=True)
            p_ref[head, these, window] = (prob * (1.0 / total)).astype(jnp.bfloat16)
        return carry

    lax.fori_loop(0, 1, probabilities, 0)
    k_ref[...] = kv_ref[0].T
    for d in range(1, share):
        gathers[1][d - 1].wait_recv()
        forwards[1][d].start()
    load_kv[1].wait()
    lax.fori_loop(1, blocks, probabilities, 0)

    left = (qt_ref, dot_ref)

    def column_sum(i, kc):
        first = max(0, kc - blocks)
        last = min(blocks - 1, kc)
        rows = slice(first * BLK, (last + 1) * BLK)
        cols = slice(kc * BLK, (kc + 1) * BLK)
        return dot(left[i][0:HD, rows], p_ref[0, rows, cols]) + dot(
            left[i][HD : 2 * HD, rows], p_ref[1, rows, cols]
        )

    def back(i, kc):
        cols = pl.ds(kc * BLK, BLK)
        return pltpu.make_async_remote_copy(
            src_ref=ret_send.at[i, :, cols],
            dst_ref=ret_recv.at[i, :, cols],
            send_sem=b_send.at[i, kc],
            recv_sem=b_recv.at[i, kc],
            device_id=(prv, tp),
            device_id_type=MESH,
        )

    backs = [[back(i, kc) for kc in range(blocks)] for i in range(2)]
    weights = (scale, 1.0)

    def send_back(i):
        for kc in range(blocks):
            cols = slice(kc * BLK, (kc + 1) * BLK)
            ret_send[i, :, cols] = (column_sum(i, kc) * weights[i]).astype(jnp.bfloat16)
            backs[i][kc].start()
        for kc in range(blocks):
            cols = slice(kc * BLK, (kc + 1) * BLK)
            total_ref[i, :, cols] = column_sum(i, kc + blocks) * weights[i]

    def scatter(i, d):
        return pltpu.make_async_remote_copy(
            src_ref=rs_send.at[i, band_of(other(d)), :],
            dst_ref=rs_recv.at[i, d - 1],
            send_sem=r_send.at[i, d - 1],
            recv_sem=r_recv.at[i, d - 1],
            device_id=(ctx, base + other(d)),
            device_id_type=MESH,
        )

    scatters = [[scatter(i, d) for d in range(1, share)] for i in range(2)]

    def add_and_scatter(i):
        for kc in range(blocks):
            cols = slice(kc * BLK, (kc + 1) * BLK)
            backs[i][kc].wait_recv()
            total = total_ref[i, :, cols] + ret_recv[i, :, cols].astype(jnp.float32)
            total_ref[i, :, cols] = total
            rs_send[i, :, cols] = total.astype(jnp.bfloat16)
        for c in scatters[i]:
            c.start()

    def finish(i):
        result = total_ref[i, band_of(place), :]
        for d in range(1, share):
            scatters[i][d - 1].wait_recv()
            result = result + rs_recv[i, d - 1].astype(jnp.float32)
        fin_ref[i] = result.astype(jnp.bfloat16)

    send_back(1)

    for d in range(share):
        forwards[1][d].wait_recv()
    v_ref[...] = kv_ref[1].T

    def score_grads(b, carry):
        off = pl.multiple_of(b * BLK, BLK)
        rows = pl.ds(off, BLK)
        window = pl.ds(off, span)
        prob = jnp.concatenate([p_ref[0, rows, window], p_ref[1, rows, window]], axis=0)
        low_out = dot(prob, v_ref[window, :]).astype(jnp.bfloat16)
        out_ref[rows, 0:HD] = low_out[0:BLK]
        out_ref[rows, HD : 2 * HD] = low_out[BLK : 2 * BLK]
        grads = heads_of(do_ref, rows)
        delta = jnp.sum(
            grads.astype(jnp.float32) * low_out.astype(jnp.float32), axis=1, keepdims=True
        )
        s_ref[...] = dot(grads, kv_ref[1, :, window])
        for r in range(0, 2 * BLK, 32):
            head, low = r // BLK, r % BLK
            these = pl.ds(off + low, 32)
            change = s_ref[r : r + 32, :] - delta[r : r + 32]
            held = p_ref[head, these, window].astype(jnp.float32)
            p_ref[head, these, window] = (held * change).astype(jnp.bfloat16)
        return carry

    lax.fori_loop(0, blocks // 2, score_grads, 0)
    add_and_scatter(1)
    lax.fori_loop(blocks // 2, blocks, score_grads, 0)
    store_out = pltpu.make_async_copy(out_ref, out_hbm, store_sem.at[0])
    store_out.start()

    send_back(0)

    def query_grads(b, carry):
        off = pl.multiple_of(b * BLK, BLK)
        rows = pl.ds(off, BLK)
        window = pl.ds(off, span)
        dscore = jnp.concatenate([p_ref[0, rows, window], p_ref[1, rows, window]], axis=0)
        low = (dot(dscore, k_ref[window, :]) * scale).astype(jnp.bfloat16)
        dq_ref[rows, 0:HD] = low[0:BLK]
        dq_ref[rows, HD : 2 * HD] = low[BLK : 2 * BLK]
        return carry

    lax.fori_loop(0, blocks // 2, query_grads, 0)
    add_and_scatter(0)
    lax.fori_loop(blocks // 2, blocks, query_grads, 0)
    store_dq = pltpu.make_async_copy(dq_ref, dq_hbm, store_sem.at[1])
    store_dq.start()

    finish(1)
    store_dv = pltpu.make_async_copy(fin_ref.at[1], dvt_hbm, store_sem.at[3])
    store_dv.start()
    finish(0)
    store_dk = pltpu.make_async_copy(fin_ref.at[0], dkt_hbm, store_sem.at[2])
    store_dk.start()

    for i in range(2):
        for c in gathers[i] + forwards[i] + backs[i] + scatters[i]:
            c.wait_send()
    for c in (store_out, store_dq, store_dv, store_dk):
        c.wait()


def on_device(queries, keys, values, grad_out, doc_lengths, *, n_ctx):
    tokens, width = queries.shape
    columns = keys.shape[1]
    share = HD // columns
    blocks = tokens // BLK
    bf16, f32 = jnp.bfloat16, jnp.float32
    anywhere = pl.BlockSpec(memory_space=pl.ANY)
    dma = pltpu.SemaphoreType.DMA
    out, dq, dkt, dvt = pl.pallas_call(
        functools.partial(kernel, n_ctx, tokens, share),
        out_shape=[
            jax.ShapeDtypeStruct((tokens, width), bf16),
            jax.ShapeDtypeStruct((tokens, width), bf16),
            jax.ShapeDtypeStruct((columns, tokens), bf16),
            jax.ShapeDtypeStruct((columns, tokens), bf16),
        ],
        in_specs=[pl.BlockSpec(memory_space=pltpu.SMEM)] + [anywhere] * 4,
        out_specs=[anywhere] * 4,
        scratch_shapes=[
            pltpu.VMEM((tokens, width), bf16),
            pltpu.VMEM((tokens, width), bf16),
            pltpu.VMEM((width, tokens), bf16),
            pltpu.VMEM((width, tokens), bf16),
            pltpu.VMEM((2, HD, 2 * tokens), bf16),
            pltpu.VMEM((2 * tokens, HD), bf16),
            pltpu.VMEM((2 * tokens, HD), bf16),
            pltpu.VMEM((tokens, 128), jnp.int32),
            pltpu.VMEM((2 * BLK, tokens + BLK), f32),
            pltpu.VMEM((2, tokens, 2 * tokens), bf16),
            pltpu.VMEM((tokens, width), bf16),
            pltpu.VMEM((tokens, width), bf16),
            pltpu.VMEM((2, HD, tokens), bf16),
            pltpu.VMEM((2, HD, tokens), bf16),
            pltpu.VMEM((2, HD, tokens), f32),
            pltpu.VMEM((2, HD, tokens), bf16),
            pltpu.VMEM((2, share - 1, columns, tokens), bf16),
            pltpu.VMEM((2, columns, tokens), bf16),
            dma((4,)),
            dma((4,)),
            dma((2, share - 1)),
            dma((2, share - 1)),
            dma((2, share)),
            dma((2, share)),
            dma((2, blocks)),
            dma((2, blocks)),
            dma((2, share - 1)),
            dma((2, share - 1)),
        ],
        compiler_params=pltpu.CompilerParams(
            collective_id=0, has_side_effects=True, vmem_limit_bytes=56 * 1024 * 1024
        ),
        cost_estimate=pl.CostEstimate(
            flops=6 * 2 * 2 * tokens * (tokens + BLK) * HD,
            bytes_accessed=4 * tokens * width * 2,
            transcendentals=2 * tokens * (tokens + BLK),
        ),
    )(doc_lengths, queries, keys.T, values.T, grad_out)
    return out, dq, dkt.T, dvt.T


def solution(mesh):
    in_specs = (P("ctx", "tp"), P("ctx", "tp"), P("ctx", "tp"), P("ctx", "tp"), P())
    out_specs = (P("ctx", "tp"), P("ctx", "tp"), P("ctx", "tp"), P("ctx", "tp"))
    return jax.shard_map(
        functools.partial(on_device, n_ctx=mesh.shape["ctx"]),
        mesh=mesh,
        in_specs=in_specs,
        out_specs=out_specs,
        check_vma=False,
    )
```

time: 129 us -> 49.9 us (0.39)
  the two profiles are of different devices: /device:TPU:46 before, /device:TPU:1 now
where the time goes in v1:
time: 49.9 us; the launch traced here: 49.7 us
  Pallas kernels  44.7 us (90%)
  local copies, waits for them, and re-layouts  4.28 us (9%)
  between operations  0.65 us (1%)
    pallas_call x1, Pallas kernels, on_device(): pl.pallas_call(functools.partial(kernel, n_ctx, tokens, share), out_shape...  44.7 us
    unnamed x10, local copies, waits for them, and re-layouts  4.28 us

profile of v1, /device:TPU:1, one launch (start us, length us, event | category | flops | bytes accessed | tf_op | source)
XLA Modules:
  0.0 49.7 jit_solution(16146476313868356675)
XLA Ops:
  0.6 44.7 %shard_map.84 = (bf16[1024,256]{1,0:T(8,128)(2,1)}, bf16[1024,256]{1,0:T(8,128)(2,1)}, bf16[32,1024]{1,0:T(8,128)(2,1)}, bf16[32,1024]{1,0:T(8,128)(2,1)}) custom-call(s32[32]{0:T(128)} %doc_ref.1, bf16[1024,256]{1,0:T(8,128)(2,1)} %q_hbm.1, bf16[32,1024]{1,0:T(8,128)(2,1)} %bitcast.6, bf16[32,1024]{1,0:T(8,128)(2,1)} %bitcast.7, bf16[1024,256]{1,0:T(8,128)(2,1)} %do_hbm.1), custom_call_target="tpu_custom_call" | custom-call | flops 4026531840 | bytes 2097152 | tf_op jit(solution)/shard_map/pallas_call | solution.py:347
  45.4 0.0 copy-start
  45.4 1.9 %copy.13 = bf16[1024,256]{1,0:T(8,128)(2,1)} copy(bf16[1024,256]{1,0:T(8,128)(2,1)} %get-tuple-element.16) | data formatting | bytes 1048576
  47.3 0.0 copy-done
  47.3 0.0 copy-start.2
  47.3 0.8 %copy.14 = bf16[1024,256]{1,0:T(8,128)(2,1)} copy(bf16[1024,256]{1,0:T(8,128)(2,1)S(1)} %copy-done) | data formatting | bytes 1048576
  48.1 0.1 copy-done.2
  48.2 0.0 copy-start.1
  48.2 0.6 %copy.15 = bf16[1024,32]{0,1:T(8,128)(2,1)} copy(bf16[1024,32]{0,1:T(8,128)(2,1)S(1)} %bitcast.5) | data formatting | bytes 131072
  48.8 0.2 copy-done.1
  49.0 0.6 %copy.16 = bf16[1024,32]{0,1:T(8,128)(2,1)} copy(bf16[1024,32]{0,1:T(8,128)(2,1)S(1)} %bitcast.4) | data formatting | bytes 131072
Async XLA Ops:
  45.4 1.9 %copy-start = (bf16[1024,256]{1,0:T(8,128)(2,1)S(1)}, bf16[1024,256]{1,0:T(8,128)(2,1)}, u32[]{:S(2)}) copy-start(bf16[1024,256]{1,0:T(8,128)(2,1)} %get-tuple-element.17) | copy-start | bytes 1572868
  47.3 0.9 %copy-start.2 = (bf16[32,1024]{1,0:T(8,128)(2,1)S(1)}, bf16[32,1024]{1,0:T(8,128)(2,1)}, u32[]{:S(2)}) copy-start(bf16[32,1024]{1,0:T(8,128)(2,1)} %get-tuple-element.10) | copy-start | bytes 196612
  48.2 0.9 %copy-start.1 = (bf16[32,1024]{1,0:T(8,128)(2,1)S(1)}, bf16[32,1024]{1,0:T(8,128)(2,1)}, u32[]{:S(2)}) copy-start(bf16[32,1024]{1,0:T(8,128)(2,1)} %get-tuple-element.11) | copy-start | bytes 196612

commit v2 on v1

v2 whole, which is shorter than its diff:
```python
import functools
import math

import jax
import jax.numpy as jnp
from jax import lax
from jax.experimental import pallas as pl
from jax.experimental.pallas import tpu as pltpu
from jax.sharding import PartitionSpec as P

HD = 128
BLK = 256
NEG_FILL = -1e30
MESH = pl.DeviceIdType.MESH


def dot(a, b):
    return jnp.dot(a, b, preferred_element_type=jnp.float32)


def kernel(
    n_ctx,
    tokens,
    share,
    doc_ref,
    q_hbm,
    kt_hbm,
    vt_hbm,
    do_hbm,
    out_ref,
    dq_ref,
    dkt_ref,
    dvt_ref,
    q_ref,
    do_ref,
    qt_ref,
    dot_ref,
    kv_ref,
    k_ref,
    v_ref,
    start_ref,
    s_ref,
    p_ref,
    delta_ref,
    max_ref,
    inv_ref,
    ret_send,
    ret_recv,
    total_ref,
    rs_send,
    rs_recv,
    load_sem,
    g_send,
    g_recv,
    f_send,
    f_recv,
    b_send,
    b_recv,
    r_send,
    r_recv,
):
    scale = 1.0 / math.sqrt(HD)
    factor = scale * math.log2(math.e)
    ctx = lax.axis_index("ctx")
    tp = lax.axis_index("tp")
    place = lax.rem(tp, share)
    base = tp - place
    band = HD // share
    nxt = lax.rem(ctx + 1, n_ctx)
    prv = lax.rem(ctx + n_ctx - 1, n_ctx)
    span = tokens + BLK
    blocks = tokens // BLK
    own = pl.ds(tokens, tokens)
    before = pl.ds(0, tokens)
    kv_hbm = (kt_hbm, vt_hbm)

    def other(d):
        return lax.rem(place + d, share)

    def band_of(index):
        return pl.ds(pl.multiple_of(index * band, band), band)

    load_q = pltpu.make_async_copy(q_hbm, q_ref, load_sem.at[0])
    load_do = pltpu.make_async_copy(do_hbm, do_ref, load_sem.at[1])
    load_kv = [
        pltpu.make_async_copy(
            kv_hbm[i], kv_ref.at[i, band_of(place), own], load_sem.at[2 + i]
        )
        for i in range(2)
    ]
    for c in [load_q, load_do] + load_kv:
        c.start()

    barrier = pltpu.get_barrier_semaphore()
    for d in range(1, share):
        pl.semaphore_signal(
            barrier, inc=1, device_id=(ctx, base + other(d)), device_id_type=MESH
        )
    for c in (nxt, prv):
        pl.semaphore_signal(barrier, inc=1, device_id=(c, tp), device_id_type=MESH)
    pl.semaphore_wait(barrier, share + 1)

    def gather(i):
        copies = [
            pltpu.make_async_remote_copy(
                src_ref=kv_hbm[i],
                dst_ref=kv_ref.at[i, band_of(place), own],
                send_sem=g_send.at[i, d - 1],
                recv_sem=g_recv.at[i, d - 1],
                device_id=(ctx, base + other(d)),
                device_id_type=MESH,
            )
            for d in range(1, share)
        ]
        return copies

    def forward(i, d):
        which = lax.rem(place - d + share, share)
        src = kv_hbm[i] if d == 0 else kv_ref.at[i, band_of(which), own]
        return pltpu.make_async_remote_copy(
            src_ref=src,
            dst_ref=kv_ref.at[i, band_of(which), before],
            send_sem=f_send.at[i, d],
            recv_sem=f_recv.at[i, d],
            device_id=(nxt, tp),
            device_id_type=MESH,
        )

    gathers = [gather(i) for i in range(2)]
    forwards = [[forward(i, d) for d in range(share)] for i in range(2)]

    for c in gathers[0]:
        c.start()
    forwards[0][0].start()

    row_base = ctx * tokens
    window_base = row_base - tokens

    ends = []
    running = doc_ref[0]
    for k in range(1, doc_ref.shape[0]):
        ends.append(running)
        running = running + doc_ref[k]
    lane = lax.broadcasted_iota(jnp.int32, (128, 128), 1)
    sub = lax.broadcasted_iota(jnp.int32, (128, 128), 0)

    def find_start(chunk, carry):
        pos = sub + (row_base + chunk * 128)
        first = jnp.zeros((128, 128), jnp.int32)
        for e in ends:
            first = jnp.where(pos >= e, e, first)
        rows = pl.ds(pl.multiple_of(chunk * 128, 128), 128)
        start_ref[rows, :] = first - window_base - lane
        return carry

    lax.fori_loop(0, tokens // 128, find_start, 0)
    load_q.wait()
    load_do.wait()

    for d in range(1, share):
        gathers[0][d - 1].wait_recv()
        forwards[0][d].start()
    for c in gathers[1]:
        c.start()
    forwards[1][0].start()
    load_kv[0].wait()
    for d in range(share):
        forwards[0][d].wait_recv()

    lane32 = lax.broadcasted_iota(jnp.int32, (32, 128), 1)
    sub32 = lax.broadcasted_iota(jnp.int32, (32, 128), 0)

    def heads_of(ref, rows):
        return jnp.concatenate([ref[rows, 0:HD], ref[rows, HD : 2 * HD]], axis=0)

    def score(b):
        rows, window = slice(b * BLK, b * BLK + BLK), slice(b * BLK, b * BLK + span)
        s_ref[b] = dot(heads_of(q_ref, rows), kv_ref[0, :, window])

    def masked(b, r, j, begin):
        low, first = r % BLK, j * 128 - tokens
        part = s_ref[b, r : r + 32, j * 128 : j * 128 + 128]
        ok = begin <= b * BLK + j * 128
        if first + 127 > low:
            ok = ok & (lane32 + first <= sub32 + low)
        return jnp.where(ok, part, NEG_FILL)

    def row_max(b):
        for r in range(0, 2 * BLK, 32):
            head, low = r // BLK, b * BLK + r % BLK
            begin = start_ref[low : low + 32, :]
            top = masked(b, r, 0, begin)
            for j in range(1, span // 128):
                top = jnp.maximum(top, masked(b, r, j, begin))
            top = jnp.max(top, axis=1, keepdims=True)
            max_ref[head, low : low + 32, :] = jnp.broadcast_to(top, (32, 128))

    def probabilities(b):
        for r in range(0, 2 * BLK, 32):
            head, low = r // BLK, b * BLK + r % BLK
            begin = start_ref[low : low + 32, :]
            top = max_ref[head, low : low + 32, :]
            total = jnp.zeros((32, 128), jnp.float32)
            for j in range(span // 128):
                prob = jnp.exp2((masked(b, r, j, begin) - top) * factor)
                total = total + prob
                cols = slice(b * BLK + j * 128, b * BLK + j * 128 + 128)
                p_ref[head, low : low + 32, cols] = prob.astype(jnp.bfloat16)
            inverse = 1.0 / jnp.sum(total, axis=1, keepdims=True)
            inv_ref[head, low : low + 32, :] = jnp.broadcast_to(inverse, (32, 128))

    def scaled_turned(src_ref, dst_ref, b):
        rows = slice(b * BLK, b * BLK + BLK)
        for h in range(2):
            cols = slice(h * HD, h * HD + HD)
            part = src_ref[rows, cols].astype(jnp.float32) * inv_ref[h, rows, :]
            dst_ref[cols, rows] = part.astype(jnp.bfloat16).T

    score(0)
    row_max(0)
    score(1)
    for b in range(blocks):
        if b + 2 < blocks:
            score(b + 2)
        if b + 1 < blocks:
            row_max(b + 1)
        probabilities(b)
        scaled_turned(do_ref, dot_ref, b)
        if b == 2:
            for d in range(1, share):
                gathers[1][d - 1].wait_recv()
                forwards[1][d].start()
            load_kv[1].wait()

    left = (qt_ref, dot_ref)
    weights = (scale, 1.0)

    def rows_of(kc):
        return range(max(0, kc - blocks), min(blocks - 1, kc) + 1)

    def column_sum(i, kc):
        rows = slice(rows_of(kc)[0] * BLK, rows_of(kc)[-1] * BLK + BLK)
        cols = slice(kc * BLK, (kc + 1) * BLK)
        total = dot(left[i][0:HD, rows], p_ref[0, rows, cols]) + dot(
            left[i][HD : 2 * HD, rows], p_ref[1, rows, cols]
        )
        return total * weights[i] if weights[i] != 1.0 else total

    def back(i, kc):
        cols = pl.ds(kc * BLK, BLK)
        return pltpu.make_async_remote_copy(
            src_ref=ret_send.at[i, :, cols],
            dst_ref=ret_recv.at[i, :, cols],
            send_sem=b_send.at[i, kc],
            recv_sem=b_recv.at[i, kc],
            device_id=(prv, tp),
            device_id_type=MESH,
        )

    def scatter(i, kc, d):
        cols = pl.ds(kc * BLK, BLK)
        return pltpu.make_async_remote_copy(
            src_ref=rs_send.at[i, band_of(other(d)), cols],
            dst_ref=rs_recv.at[i, d - 1, :, cols],
            send_sem=r_send.at[i, kc, d - 1],
            recv_sem=r_recv.at[i, kc, d - 1],
            device_id=(ctx, base + other(d)),
            device_id_type=MESH,
        )

    backs = [[back(i, kc) for kc in range(blocks)] for i in range(2)]
    scatters = [
        [[scatter(i, kc, d) for d in range(1, share)] for kc in range(blocks)] for i in range(2)
    ]

    def send_back(i, kc):
        ret_send[i, :, kc * BLK : (kc + 1) * BLK] = column_sum(i, kc).astype(jnp.bfloat16)
        backs[i][kc].start()

    def add_and_scatter(i, kc, mine):
        cols = slice(kc * BLK, (kc + 1) * BLK)
        backs[i][kc].wait_recv()
        total = mine + ret_recv[i, :, cols].astype(jnp.float32)
        total_ref[i, :, cols] = total
        rs_send[i, :, cols] = total.astype(jnp.bfloat16)
        for c in scatters[i][kc]:
            c.start()

    def finish(i):
        for kc in range(blocks):
            for c in scatters[i][kc]:
                c.wait_recv()
        result = total_ref[i, band_of(place), :]
        for d in range(1, share):
            result = result + rs_recv[i, d - 1].astype(jnp.float32)
        (dkt_ref, dvt_ref)[i][...] = result.astype(jnp.bfloat16)

    for kc in range(blocks):
        send_back(1, kc)
    for kc in range(blocks):
        total_ref[1, :, kc * BLK : (kc + 1) * BLK] = column_sum(1, kc + blocks)

    for d in range(share):
        forwards[1][d].wait_recv()
    v_ref[...] = kv_ref[1].T

    def outputs(b):
        rows, window = slice(b * BLK, b * BLK + BLK), slice(b * BLK, b * BLK + span)
        prob = jnp.concatenate([p_ref[0, rows, window], p_ref[1, rows, window]], axis=0)
        sums = dot(prob, v_ref[window, :])
        for h in range(2):
            part = (sums[h * BLK : h * BLK + BLK] * inv_ref[h, rows, :]).astype(jnp.bfloat16)
            out_ref[rows, h * HD : h * HD + HD] = part
            grads = do_ref[rows, h * HD : h * HD + HD].astype(jnp.float32)
            delta = jnp.sum(grads * part.astype(jnp.float32), axis=1, keepdims=True)
            delta_ref[h, rows, :] = jnp.broadcast_to(delta, (BLK, 128))

    for b in range(blocks):
        outputs(b)
        if b == 1:
            for kc in range(blocks):
                add_and_scatter(1, kc, total_ref[1, :, kc * BLK : (kc + 1) * BLK])

    k_ref[...] = kv_ref[0].T
    for b in range(blocks):
        scaled_turned(q_ref, qt_ref, b)

    def score_grads(b, kc):
        rows, cols = slice(b * BLK, b * BLK + BLK), slice(kc * BLK, kc * BLK + BLK)
        change = dot(heads_of(do_ref, rows), kv_ref[1, :, cols])
        for r in range(0, 2 * BLK, 64):
            head, low = r // BLK, r % BLK
            these = slice(b * BLK + low, b * BLK + low + 64)
            delta = delta_ref[head, these, :]
            delta = jnp.concatenate([delta] * (BLK // 128), axis=1)
            held = p_ref[head, these, cols].astype(jnp.float32)
            p_ref[head, these, cols] = (held * (change[r : r + 64] - delta)).astype(jnp.bfloat16)

    for kc in range(2 * blocks):
        for b in rows_of(kc):
            score_grads(b, kc)
        if kc < blocks:
            send_back(0, kc)
        else:
            add_and_scatter(0, kc - blocks, column_sum(0, kc))

    finish(1)

    for b in range(blocks):
        rows, window = slice(b * BLK, b * BLK + BLK), slice(b * BLK, b * BLK + span)
        dscore = jnp.concatenate([p_ref[0, rows, window], p_ref[1, rows, window]], axis=0)
        sums = dot(dscore, k_ref[window, :])
        for h in range(2):
            part = sums[h * BLK : h * BLK + BLK] * (inv_ref[h, rows, :] * scale)
            dq_ref[rows, h * HD : h * HD + HD] = part.astype(jnp.bfloat16)

    finish(0)

    for i in range(2):
        for c in gathers[i] + forwards[i] + backs[i] + sum(scatters[i], []):
            c.wait_send()


def hand_over(*refs):
    count = len(refs) // 2
    sems = refs[-1]
    copies = [
        pltpu.make_async_copy(refs[i], refs[count + i], sems.at[i]) for i in range(count)
    ]
    for c in copies:
        c.start()
    for c in copies:
        c.wait()


def on_device(queries, keys, values, grad_out, doc_lengths, *, n_ctx):
    tokens, width = queries.shape
    columns = keys.shape[1]
    share = HD // columns
    blocks = tokens // BLK
    bf16, f32 = jnp.bfloat16, jnp.float32
    anywhere = pl.BlockSpec(memory_space=pltpu.HBM)
    dma = pltpu.SemaphoreType.DMA
    shapes = [(tokens, width), (tokens, width), (columns, tokens), (columns, tokens)]
    results = pl.pallas_call(
        functools.partial(kernel, n_ctx, tokens, share),
        out_shape=[pltpu.VMEM(shape, bf16) for shape in shapes],
        in_specs=[pl.BlockSpec(memory_space=pltpu.SMEM)] + [anywhere] * 4,
        out_specs=[pl.BlockSpec(memory_space=pltpu.VMEM)] * 4,
        scratch_shapes=[
            pltpu.VMEM((tokens, width), bf16),
            pltpu.VMEM((tokens, width), bf16),
            pltpu.VMEM((width, tokens), bf16),
            pltpu.VMEM((width, tokens), bf16),
            pltpu.VMEM((2, HD, 2 * tokens), bf16),
            pltpu.VMEM((2 * tokens, HD), bf16),
            pltpu.VMEM((2 * tokens, HD), bf16),
            pltpu.VMEM((tokens, 128), jnp.int32),
            pltpu.VMEM((blocks, 2 * BLK, tokens + BLK), f32),
            pltpu.VMEM((2, tokens, 2 * tokens), bf16),
            pltpu.VMEM((2, tokens, 128), f32),
            pltpu.VMEM((2, tokens, 128), f32),
            pltpu.VMEM((2, tokens, 128), f32),
            pltpu.VMEM((2, HD, tokens), bf16),
            pltpu.VMEM((2, HD, tokens), bf16),
            pltpu.VMEM((2, HD, tokens), f32),
            pltpu.VMEM((2, HD, tokens), bf16),
            pltpu.VMEM((2, share - 1, columns, tokens), bf16),
            dma((4,)),
            dma((2, share - 1)),
            dma((2, share - 1)),
            dma((2, share)),
            dma((2, share)),
            dma((2, blocks)),
            dma((2, blocks)),
            dma((2, blocks, share - 1)),
            dma((2, blocks, share - 1)),
        ],
        compiler_params=pltpu.CompilerParams(
            collective_id=0, has_side_effects=True, vmem_limit_bytes=60 * 1024 * 1024
        ),
        cost_estimate=pl.CostEstimate(
            flops=6 * 2 * 2 * tokens * (tokens + BLK) * HD,
            bytes_accessed=4 * tokens * width * 2,
            transcendentals=2 * tokens * (tokens + BLK),
        ),
    )(doc_lengths, queries, keys.T, values.T, grad_out)
    out, dq, dkt, dvt = pl.pallas_call(
        hand_over,
        out_shape=[jax.ShapeDtypeStruct(shape, bf16) for shape in shapes],
        in_specs=[pl.BlockSpec(memory_space=pltpu.VMEM)] * 4,
        out_specs=[anywhere] * 4,
        scratch_shapes=[dma((4,))],
        compiler_params=pltpu.CompilerParams(vmem_limit_bytes=4 * 1024 * 1024),
        cost_estimate=pl.CostEstimate(
            flops=0, bytes_accessed=2 * tokens * width * 2, transcendentals=0
        ),
    )(*results)
    return out, dq, dkt.T, dvt.T


def solution(mesh):
    in_specs = (P("ctx", "tp"), P("ctx", "tp"), P("ctx", "tp"), P("ctx", "tp"), P())
    out_specs = (P("ctx", "tp"), P("ctx", "tp"), P("ctx", "tp"), P("ctx", "tp"))
    return jax.shard_map(
        functools.partial(on_device, n_ctx=mesh.shape["ctx"]),
        mesh=mesh,
        in_specs=in_specs,
        out_specs=out_specs,
        check_vma=False,
    )
```

time: 49.9 us -> 41.8 us (0.84)
  local copies, waits for them, and re-layouts: 4.28 us -> 0 us
  Pallas kernels: 44.7 us -> 40.5 us
    pallas_call x1, Pallas kernels: 44.7 us -> 39.5 us  [on_device(): pl.pallas_call(functools.partial(kernel, n_ctx, tokens, share), out_shape...]
    unnamed x10 -> x0, local copies, waits for them, and re-layouts: 4.28 us -> none
    pallas_call x0 -> x1, Pallas kernels: none -> 1.03 us  [on_device(): pl.pallas_call(hand_over, out_shape=[jax.ShapeDtypeStruct(shape, bf16) fo...]
where the time goes in v2:
time: 41.8 us; the launch traced here: 41.2 us
  Pallas kernels  40.5 us (97%)
  between operations  0.64 us (2%)
    pallas_call x1, Pallas kernels, on_device(): pl.pallas_call(functools.partial(kernel, n_ctx, tokens, share), out_shape...  39.5 us
    pallas_call x1, Pallas kernels, on_device(): pl.pallas_call(hand_over, out_shape=[jax.ShapeDtypeStruct(shape, bf16) fo...  1.03 us

profile of v2, /device:TPU:1, one launch (start us, length us, event | category | flops | bytes accessed | tf_op | source)
XLA Modules:
  0.0 41.2 jit_solution(9011655915617605337)
XLA Ops:
  0.6 39.5 %shard_map.84 = (bf16[1024,256]{1,0:T(8,128)(2,1)S(1)}, bf16[1024,256]{1,0:T(8,128)(2,1)S(1)}, bf16[32,1024]{1,0:T(8,128)(2,1)S(1)}, bf16[32,1024]{1,0:T(8,128)(2,1)S(1)}) custom-call(s32[32]{0:T(128)} %doc_ref.1, bf16[1024,256]{1,0:T(8,128)(2,1)} %q_hbm.1, bf16[32,1024]{1,0:T(8,128)(2,1)} %bitcast.4, bf16[32,1024]{1,0:T(8,128)(2,1)} %bitcast.5, ...), custom_call_target="tpu_custom_call" | custom-call | flops 4026531840 | bytes 2097152 | tf_op jit(solution)/shard_map/pallas_call | solution.py:385
  40.1 1.0 %shard_map.85 = (bf16[1024,256]{1,0:T(8,128)(2,1)}, bf16[1024,256]{1,0:T(8,128)(2,1)}, bf16[32,1024]{1,0:T(8,128)(2,1)}, bf16[32,1024]{1,0:T(8,128)(2,1)}) custom-call(bf16[1024,256]{1,0:T(8,128)(2,1)S(1)} %get-tuple-element.12.refs_0_, bf16[1024,256]{1,0:T(8,128)(2,1)S(1)} %get-tuple-element.13.refs_1_, bf16[32,1024]{1,0:T(8,128)(2,1)S(1)} %get-tuple-element.14.refs_2_, ...), custom_call_target="tpu_custom_call" | custom-call | bytes 1048576 | tf_op jit(solution)/shard_map/pallas_call | solution.py:428

commit v3 on v2

--- a/solution.py
+++ b/solution.py
@@ -74,8 +74,16 @@
     before = pl.ds(0, tokens)
     kv_hbm = (kt_hbm, vt_hbm)
 
+    in_middle = lax.rem((place + 1) // 2, 2) == 1
+    others = (
+        place,
+        place + 1 - 2 * lax.rem(place, 2),
+        place + 2 - 4 * (place // 2),
+        share - 1 - place,
+    )
+
     def other(d):
-        return lax.rem(place + d, share)
+        return others[d]
 
     def band_of(index):
         return pl.ds(pl.multiple_of(index * band, band), band)
@@ -100,38 +108,44 @@
         pl.semaphore_signal(barrier, inc=1, device_id=(c, tp), device_id_type=MESH)
     pl.semaphore_wait(barrier, share + 1)
 
-    def gather(i):
-        copies = [
-            pltpu.make_async_remote_copy(
-                src_ref=kv_hbm[i],
-                dst_ref=kv_ref.at[i, band_of(place), own],
-                send_sem=g_send.at[i, d - 1],
-                recv_sem=g_recv.at[i, d - 1],
-                device_id=(ctx, base + other(d)),
-                device_id_type=MESH,
-            )
-            for d in range(1, share)
-        ]
-        return copies
+    def gather(i, d, source):
+        return pltpu.make_async_remote_copy(
+            src_ref=kv_hbm[i] if source == 0 else kv_ref.at[i, band_of(other(2)), own],
+            dst_ref=kv_ref.at[i, band_of(other(source)), own],
+            send_sem=g_send.at[i, 3 if source else d - 1],
+            recv_sem=g_recv.at[i, 2 if source else d - 1],
+            device_id=(ctx, base + other(d)),
+            device_id_type=MESH,
+        )
 
     def forward(i, d):
-        which = lax.rem(place - d + share, share)
-        src = kv_hbm[i] if d == 0 else kv_ref.at[i, band_of(which), own]
+        src = kv_hbm[i] if d == 0 else kv_ref.at[i, band_of(other(d)), own]
         return pltpu.make_async_remote_copy(
             src_ref=src,
-            dst_ref=kv_ref.at[i, band_of(which), before],
+            dst_ref=kv_ref.at[i, band_of(other(d)), before],
             send_sem=f_send.at[i, d],
             recv_sem=f_recv.at[i, d],
             device_id=(nxt, tp),
             device_id_type=MESH,
         )
 
-    gathers = [gather(i) for i in range(2)]
+    gathers = [[gather(i, d, 0) for d in range(1, share)] for i in range(2)]
+    relays = [gather(i, 1, 2) for i in range(2)]
     forwards = [[forward(i, d) for d in range(share)] for i in range(2)]
 
-    for c in gathers[0]:
-        c.start()
-    forwards[0][0].start()
+    def send_own(i):
+        gathers[i][1].start()
+        pl.when(in_middle)(gathers[i][2].start)
+        gathers[i][0].start()
+        forwards[i][0].start()
+
+    def receive(i, d):
+        gathers[i][d - 1].wait_recv()
+        if d == 2:
+            pl.when(in_middle)(relays[i].start)
+        forwards[i][d].start()
+
+    send_own(0)
 
     row_base = ctx * tokens
     window_base = row_base - tokens
@@ -157,15 +171,14 @@
     load_q.wait()
     load_do.wait()
 
-    for d in range(1, share):
-        gathers[0][d - 1].wait_recv()
-        forwards[0][d].start()
-    for c in gathers[1]:
-        c.start()
-    forwards[1][0].start()
+    receive(0, 2)
+    receive(0, 1)
+    send_own(1)
+    receive(0, 3)
     load_kv[0].wait()
     for d in range(share):
         forwards[0][d].wait_recv()
+    receive(1, 2)
 
     lane32 = lax.broadcasted_iota(jnp.int32, (32, 128), 1)
     sub32 = lax.broadcasted_iota(jnp.int32, (32, 128), 0)
@@ -227,9 +240,8 @@
         probabilities(b)
         scaled_turned(do_ref, dot_ref, b)
         if b == 2:
-            for d in range(1, share):
-                gathers[1][d - 1].wait_recv()
-                forwards[1][d].start()
+            receive(1, 1)
+            receive(1, 3)
             load_kv[1].wait()
 
     left = (qt_ref, dot_ref)
@@ -257,20 +269,25 @@
             device_id_type=MESH,
         )
 
+    def straight(i, kc):
+        return i == 0 and kc == blocks - 1
+
     def scatter(i, kc, d):
         cols = pl.ds(kc * BLK, BLK)
+        target, slot = (1, 3) if d == share else (d, d - 1)
         return pltpu.make_async_remote_copy(
-            src_ref=rs_send.at[i, band_of(other(d)), cols],
-            dst_ref=rs_recv.at[i, d - 1, :, cols],
-            send_sem=r_send.at[i, kc, d - 1],
-            recv_sem=r_recv.at[i, kc, d - 1],
-            device_id=(ctx, base + other(d)),
+            src_ref=rs_send.at[i, band_of(other(min(d, share - 1))), cols],
+            dst_ref=rs_recv.at[i, slot, :, cols],
+            send_sem=r_send.at[i, kc, slot],
+            recv_sem=r_recv.at[i, kc, slot],
+            device_id=(ctx, base + other(target)),
             device_id_type=MESH,
         )
 
     backs = [[back(i, kc) for kc in range(blocks)] for i in range(2)]
     scatters = [
-        [[scatter(i, kc, d) for d in range(1, share)] for kc in range(blocks)] for i in range(2)
+        [[scatter(i, kc, d) for d in range(1, share + 1)] for kc in range(blocks)]
+        for i in range(2)
     ]
 
     def send_back(i, kc):
@@ -283,17 +300,79 @@
         total = mine + ret_recv[i, :, cols].astype(jnp.float32)
         total_ref[i, :, cols] = total
         rs_send[i, :, cols] = total.astype(jnp.bfloat16)
-        for c in scatters[i][kc]:
-            c.start()
+        first, second, third, relay = scatters[i][kc]
+        if straight(i, kc):
+            second.start()
+            third.start()
+            first.start()
+        else:
+
+            @pl.when(in_middle)
+            def _():
+                third.start()
+
+            @pl.when(jnp.logical_not(in_middle))
+            def _():
+                relay.start()
+                second.start()
+
+            first.start()
+
+    def add_on_the_way(i, kc):
+        if straight(i, kc):
+            return
+        cols = slice(kc * BLK, (kc + 1) * BLK)
+
+        @pl.when(in_middle)
+        def _():
+            scatters[i][kc][3].wait_recv()
+            total = total_ref[i, band_of(other(2)), cols]
+            total = total + rs_recv[i, 3, :, cols].astype(jnp.float32)
+            rs_send[i, band_of(other(2)), cols] = total.astype(jnp.bfloat16)
+            scatters[i][kc][1].start()
 
     def finish(i):
         for kc in range(blocks):
-            for c in scatters[i][kc]:
-                c.wait_recv()
+            cols = slice(kc * BLK, (kc + 1) * BLK)
+
+            def add_third(kc=kc, cols=cols):
+                scatters[i][kc][2].wait_recv()
+                total_ref[i, band_of(place), cols] += rs_recv[i, 2, :, cols].astype(jnp.float32)
+
+            scatters[i][kc][0].wait_recv()
+            scatters[i][kc][1].wait_recv()
+            if straight(i, kc):
+                add_third()
+            else:
+                pl.when(in_middle)(add_third)
         result = total_ref[i, band_of(place), :]
-        for d in range(1, share):
+        for d in range(1, share - 1):
             result = result + rs_recv[i, d - 1].astype(jnp.float32)
         (dkt_ref, dvt_ref)[i][...] = result.astype(jnp.bfloat16)
+
+    def all_sent(i):
+        first = gathers[i][:2] + forwards[i] + backs[i]
+        in_the_middle = [gathers[i][2], relays[i]]
+        at_the_ends = []
+        for kc in range(blocks):
+            first += scatters[i][kc][:2]
+            if straight(i, kc):
+                first.append(scatters[i][kc][2])
+            else:
+                in_the_middle.append(scatters[i][kc][2])
+                at_the_ends.append(scatters[i][kc][3])
+        for c in first:
+            c.wait_send()
+
+        @pl.when(in_middle)
+        def _():
+            for c in in_the_middle:
+                c.wait_send()
+
+        @pl.when(jnp.logical_not(in_middle))
+        def _():
+            for c in at_the_ends:
+                c.wait_send()
 
     for kc in range(blocks):
         send_back(1, kc)
@@ -320,6 +399,8 @@
         if b == 1:
             for kc in range(blocks):
                 add_and_scatter(1, kc, total_ref[1, :, kc * BLK : (kc + 1) * BLK])
+    for kc in range(blocks):
+        add_on_the_way(1, kc)
 
     k_ref[...] = kv_ref[0].T
     for b in range(blocks):
@@ -343,6 +424,8 @@
             send_back(0, kc)
         else:
             add_and_scatter(0, kc - blocks, column_sum(0, kc))
+            if kc > blocks:
+                add_on_the_way(0, kc - blocks - 1)
 
     finish(1)
 
@@ -357,8 +440,7 @@
     finish(0)
 
     for i in range(2):
-        for c in gathers[i] + forwards[i] + backs[i] + sum(scatters[i], []):
-            c.wait_send()
+        all_sent(i)
 
 
 def hand_over(*refs):
@@ -405,16 +487,16 @@
             pltpu.VMEM((2, HD, tokens), bf16),
             pltpu.VMEM((2, HD, tokens), f32),
             pltpu.VMEM((2, HD, tokens), bf16),
-            pltpu.VMEM((2, share - 1, columns, tokens), bf16),
+            pltpu.VMEM((2, share, columns, tokens), bf16),
             dma((4,)),
-            dma((2, share - 1)),
+            dma((2, share)),
             dma((2, share - 1)),
             dma((2, share)),
             dma((2, share)),
             dma((2, blocks)),
             dma((2, blocks)),
-            dma((2, blocks, share - 1)),
-            dma((2, blocks, share - 1)),
+            dma((2, blocks, share)),
+            dma((2, blocks, share)),
         ],
         compiler_params=pltpu.CompilerParams(
             collective_id=0, has_side_effects=True, vmem_limit_bytes=60 * 1024 * 1024

time: 41.8 us -> 44.2 us (1.057); the launches traced: 41.2 us -> 44 us
  Pallas kernels: 40.5 us -> 43.4 us
    pallas_call x1, Pallas kernels: 39.5 us -> 42.4 us  [on_device(): pl.pallas_call(functools.partial(kernel, n_ctx, tokens, share), out_shape...]
where the time goes in v3:
time: 44.2 us; the launch traced here: 44 us
  Pallas kernels  43.4 us (98%)
  between operations  0.64 us (1%)
    pallas_call x1, Pallas kernels, on_device(): pl.pallas_call(functools.partial(kernel, n_ctx, tokens, share), out_shape...  42.4 us
    pallas_call x1, Pallas kernels, on_device(): pl.pallas_call(hand_over, out_shape=[jax.ShapeDtypeStruct(shape, bf16) fo...  1.03 us

profile of v3, /device:TPU:1, one launch (start us, length us, event | category | flops | bytes accessed | tf_op | source)
XLA Modules:
  0.0 44.0 jit_solution(16905802054416321484)
XLA Ops:
  0.6 42.4 %shard_map.84 = (bf16[1024,256]{1,0:T(8,128)(2,1)S(1)}, bf16[1024,256]{1,0:T(8,128)(2,1)S(1)}, bf16[32,1024]{1,0:T(8,128)(2,1)S(1)}, bf16[32,1024]{1,0:T(8,128)(2,1)S(1)}) custom-call(s32[32]{0:T(128)} %doc_ref.1, bf16[1024,256]{1,0:T(8,128)(2,1)} %q_hbm.1, bf16[32,1024]{1,0:T(8,128)(2,1)} %bitcast.4, bf16[32,1024]{1,0:T(8,128)(2,1)} %bitcast.5, ...), custom_call_target="tpu_custom_call" | custom-call | flops 4026531840 | bytes 2097152 | tf_op jit(solution)/shard_map/pallas_call | solution.py:467
  43.0 1.0 %shard_map.85 = (bf16[1024,256]{1,0:T(8,128)(2,1)}, bf16[1024,256]{1,0:T(8,128)(2,1)}, bf16[32,1024]{1,0:T(8,128)(2,1)}, bf16[32,1024]{1,0:T(8,128)(2,1)}) custom-call(bf16[1024,256]{1,0:T(8,128)(2,1)S(1)} %get-tuple-element.12.refs_0_, bf16[1024,256]{1,0:T(8,128)(2,1)S(1)} %get-tuple-element.13.refs_1_, bf16[32,1024]{1,0:T(8,128)(2,1)S(1)} %get-tuple-element.14.refs_2_, ...), custom_call_target="tpu_custom_call" | custom-call | bytes 1048576 | tf_op jit(solution)/shard_map/pallas_call | solution.py:510

commit v4 on v2

--- a/solution.py
+++ b/solution.py
@@ -157,15 +157,15 @@
     load_q.wait()
     load_do.wait()
 
-    for d in range(1, share):
-        gathers[0][d - 1].wait_recv()
-        forwards[0][d].start()
+    for c in gathers[0]:
+        c.wait_send()
     for c in gathers[1]:
         c.start()
     forwards[1][0].start()
     load_kv[0].wait()
-    for d in range(share):
-        forwards[0][d].wait_recv()
+    for d in range(1, share):
+        gathers[0][d - 1].wait_recv()
+        forwards[0][d].start()
 
     lane32 = lax.broadcasted_iota(jnp.int32, (32, 128), 1)
     sub32 = lax.broadcasted_iota(jnp.int32, (32, 128), 0)
@@ -173,9 +173,12 @@
     def heads_of(ref, rows):
         return jnp.concatenate([ref[rows, 0:HD], ref[rows, HD : 2 * HD]], axis=0)
 
-    def score(b):
-        rows, window = slice(b * BLK, b * BLK + BLK), slice(b * BLK, b * BLK + span)
-        s_ref[b] = dot(heads_of(q_ref, rows), kv_ref[0, :, window])
+    def middle(b):
+        return tokens - b * BLK
+
+    def score(b, first, last):
+        rows, cols = slice(b * BLK, b * BLK + BLK), slice(b * BLK + first, b * BLK + last)
+        s_ref[b, :, first:last] = dot(heads_of(q_ref, rows), kv_ref[0, :, cols])
 
     def masked(b, r, j, begin):
         low, first = r % BLK, j * 128 - tokens
@@ -185,12 +188,21 @@
             ok = ok & (lane32 + first <= sub32 + low)
         return jnp.where(ok, part, NEG_FILL)
 
+    def own_max(b):
+        for r in range(0, 2 * BLK, 32):
+            head, low = r // BLK, b * BLK + r % BLK
+            begin = start_ref[low : low + 32, :]
+            top = masked(b, r, middle(b) // 128, begin)
+            for j in range(middle(b) // 128 + 1, span // 128):
+                top = jnp.maximum(top, masked(b, r, j, begin))
+            max_ref[head, low : low + 32, :] = top
+
     def row_max(b):
         for r in range(0, 2 * BLK, 32):
             head, low = r // BLK, b * BLK + r % BLK
             begin = start_ref[low : low + 32, :]
-            top = masked(b, r, 0, begin)
-            for j in range(1, span // 128):
+            top = max_ref[head, low : low + 32, :]
+            for j in range(middle(b) // 128):
                 top = jnp.maximum(top, masked(b, r, j, begin))
             top = jnp.max(top, axis=1, keepdims=True)
             max_ref[head, low : low + 32, :] = jnp.broadcast_to(top, (32, 128))
@@ -216,22 +228,6 @@
             part = src_ref[rows, cols].astype(jnp.float32) * inv_ref[h, rows, :]
             dst_ref[cols, rows] = part.astype(jnp.bfloat16).T
 
-    score(0)
-    row_max(0)
-    score(1)
-    for b in range(blocks):
-        if b + 2 < blocks:
-            score(b + 2)
-        if b + 1 < blocks:
-            row_max(b + 1)
-        probabilities(b)
-        scaled_turned(do_ref, dot_ref, b)
-        if b == 2:
-            for d in range(1, share):
-                gathers[1][d - 1].wait_recv()
-                forwards[1][d].start()
-            load_kv[1].wait()
-
     left = (qt_ref, dot_ref)
     weights = (scale, 1.0)
 
@@ -257,52 +253,83 @@
             device_id_type=MESH,
         )
 
-    def scatter(i, kc, d):
-        cols = pl.ds(kc * BLK, BLK)
+    pieces = ((1,) * blocks, (blocks // 2,) * 2)
+
+    def scatter(i, piece, d):
+        size = pieces[i][piece] * BLK
+        cols = pl.ds(sum(pieces[i][:piece]) * BLK, size)
         return pltpu.make_async_remote_copy(
             src_ref=rs_send.at[i, band_of(other(d)), cols],
             dst_ref=rs_recv.at[i, d - 1, :, cols],
-            send_sem=r_send.at[i, kc, d - 1],
-            recv_sem=r_recv.at[i, kc, d - 1],
+            send_sem=r_send.at[i, piece, d - 1],
+            recv_sem=r_recv.at[i, piece, d - 1],
             device_id=(ctx, base + other(d)),
             device_id_type=MESH,
         )
 
     backs = [[back(i, kc) for kc in range(blocks)] for i in range(2)]
     scatters = [
-        [[scatter(i, kc, d) for d in range(1, share)] for kc in range(blocks)] for i in range(2)
+        [[scatter(i, piece, d) for d in range(1, share)] for piece in range(len(pieces[i]))]
+        for i in range(2)
     ]
 
-    def send_back(i, kc):
+    def column_back(i, kc):
         ret_send[i, :, kc * BLK : (kc + 1) * BLK] = column_sum(i, kc).astype(jnp.bfloat16)
-        backs[i][kc].start()
-
-    def add_and_scatter(i, kc, mine):
+
+    def add_returned(i, kc, mine):
         cols = slice(kc * BLK, (kc + 1) * BLK)
         backs[i][kc].wait_recv()
         total = mine + ret_recv[i, :, cols].astype(jnp.float32)
         total_ref[i, :, cols] = total
         rs_send[i, :, cols] = total.astype(jnp.bfloat16)
-        for c in scatters[i][kc]:
-            c.start()
 
     def finish(i):
-        for kc in range(blocks):
-            for c in scatters[i][kc]:
+        for piece in scatters[i]:
+            for c in piece:
                 c.wait_recv()
         result = total_ref[i, band_of(place), :]
         for d in range(1, share):
             result = result + rs_recv[i, d - 1].astype(jnp.float32)
         (dkt_ref, dvt_ref)[i][...] = result.astype(jnp.bfloat16)
 
-    for kc in range(blocks):
-        send_back(1, kc)
+    score(0, middle(0), span)
+    for b in range(blocks):
+        if b + 1 < blocks:
+            score(b + 1, middle(b + 1), span)
+        own_max(b)
+    for d in range(share):
+        forwards[0][d].wait_recv()
+
+    score(0, 0, middle(0))
+    row_max(0)
+    score(1, 0, middle(1))
+    for b in range(blocks):
+        if b + 2 < blocks:
+            score(b + 2, 0, middle(b + 2))
+        if b + 1 < blocks:
+            row_max(b + 1)
+        if b:
+            column_back(1, b - 1)
+        probabilities(b)
+        scaled_turned(do_ref, dot_ref, b)
+        if b:
+            backs[1][b - 1].start()
+        if b == 2:
+            for d in range(1, share):
+                gathers[1][d - 1].wait_recv()
+                forwards[1][d].start()
+            load_kv[1].wait()
+
+    column_back(1, blocks - 1)
+    backs[1][blocks - 1].start()
     for kc in range(blocks):
         total_ref[1, :, kc * BLK : (kc + 1) * BLK] = column_sum(1, kc + blocks)
-
+    for b in range(blocks):
+        scaled_turned(q_ref, qt_ref, b)
+    v_ref[own, :] = kv_ref[1, :, own].T
     for d in range(share):
         forwards[1][d].wait_recv()
-    v_ref[...] = kv_ref[1].T
+    v_ref[before, :] = kv_ref[1, :, before].T
 
     def outputs(b):
         rows, window = slice(b * BLK, b * BLK + BLK), slice(b * BLK, b * BLK + span)
@@ -317,13 +344,12 @@
 
     for b in range(blocks):
         outputs(b)
-        if b == 1:
+        if b == 0:
             for kc in range(blocks):
-                add_and_scatter(1, kc, total_ref[1, :, kc * BLK : (kc + 1) * BLK])
-
-    k_ref[...] = kv_ref[0].T
-    for b in range(blocks):
-        scaled_turned(q_ref, qt_ref, b)
+                add_returned(1, kc, total_ref[1, :, kc * BLK : (kc + 1) * BLK])
+                if kc % 2:
+                    for c in scatters[1][kc // 2]:
+                        c.start()
 
     def score_grads(b, kc):
         rows, cols = slice(b * BLK, b * BLK + BLK), slice(kc * BLK, kc * BLK + BLK)
@@ -336,14 +362,21 @@
             held = p_ref[head, these, cols].astype(jnp.float32)
             p_ref[head, these, cols] = (held * (change[r : r + 64] - delta)).astype(jnp.bfloat16)
 
+    for b in rows_of(0):
+        score_grads(b, 0)
     for kc in range(2 * blocks):
-        for b in rows_of(kc):
-            score_grads(b, kc)
+        if kc + 1 < 2 * blocks:
+            for b in rows_of(kc + 1):
+                score_grads(b, kc + 1)
         if kc < blocks:
-            send_back(0, kc)
+            column_back(0, kc)
+            backs[0][kc].start()
         else:
-            add_and_scatter(0, kc - blocks, column_sum(0, kc))
-
+            add_returned(0, kc - blocks, column_sum(0, kc))
+            for c in scatters[0][kc - blocks]:
+                c.start()
+
+    k_ref[...] = kv_ref[0].T
     finish(1)
 
     for b in range(blocks):
@@ -357,7 +390,7 @@
     finish(0)
 
     for i in range(2):
-        for c in gathers[i] + forwards[i] + backs[i] + sum(scatters[i], []):
+        for c in (gathers[i] if i else []) + forwards[i] + backs[i] + sum(scatters[i], []):
             c.wait_send()
 
 

time: 41.8 us -> 43 us (1.029); the launches traced: 41.2 us -> 42.9 us
  Pallas kernels: 40.5 us -> 42.2 us
    pallas_call x1, Pallas kernels: 39.5 us -> 41.2 us  [on_device(): pl.pallas_call(functools.partial(kernel, n_ctx, tokens, share), out_shape...]
where the time goes in v4:
time: 43 us; the launch traced here: 42.9 us
  Pallas kernels  42.2 us (98%)
  between operations  0.64 us (1%)
    pallas_call x1, Pallas kernels, on_device(): pl.pallas_call(functools.partial(kernel, n_ctx, tokens, share), out_shape...  41.2 us
    pallas_call x1, Pallas kernels, on_device(): pl.pallas_call(hand_over, out_shape=[jax.ShapeDtypeStruct(shape, bf16) fo...  1.03 us

profile of v4, /device:TPU:1, one launch (start us, length us, event | category | flops | bytes accessed | tf_op | source)
XLA Modules:
  0.0 42.9 jit_solution(14281448100718080494)
XLA Ops:
  0.6 41.2 %shard_map.84 = (bf16[1024,256]{1,0:T(8,128)(2,1)S(1)}, bf16[1024,256]{1,0:T(8,128)(2,1)S(1)}, bf16[32,1024]{1,0:T(8,128)(2,1)S(1)}, bf16[32,1024]{1,0:T(8,128)(2,1)S(1)}) custom-call(s32[32]{0:T(128)} %doc_ref.1, bf16[1024,256]{1,0:T(8,128)(2,1)} %q_hbm.1, bf16[32,1024]{1,0:T(8,128)(2,1)} %bitcast.4, bf16[32,1024]{1,0:T(8,128)(2,1)} %bitcast.5, ...), custom_call_target="tpu_custom_call" | custom-call | flops 4026531840 | bytes 2097152 | tf_op jit(solution)/shard_map/pallas_call | solution.py:418
  41.9 1.0 %shard_map.85 = (bf16[1024,256]{1,0:T(8,128)(2,1)}, bf16[1024,256]{1,0:T(8,128)(2,1)}, bf16[32,1024]{1,0:T(8,128)(2,1)}, bf16[32,1024]{1,0:T(8,128)(2,1)}) custom-call(bf16[1024,256]{1,0:T(8,128)(2,1)S(1)} %get-tuple-element.12.refs_0_, bf16[1024,256]{1,0:T(8,128)(2,1)S(1)} %get-tuple-element.13.refs_1_, bf16[32,1024]{1,0:T(8,128)(2,1)S(1)} %get-tuple-element.14.refs_2_, ...), custom_call_target="tpu_custom_call" | custom-call | bytes 1048576 | tf_op jit(solution)/shard_map/pallas_call | solution.py:461

commit v5 on v4

--- a/solution.py
+++ b/solution.py
@@ -38,7 +38,7 @@
     kv_ref,
     k_ref,
     v_ref,
-    start_ref,
+    bias_ref,
     s_ref,
     p_ref,
     delta_ref,
@@ -150,7 +150,13 @@
         for e in ends:
             first = jnp.where(pos >= e, e, first)
         rows = pl.ds(pl.multiple_of(chunk * 128, 128), 128)
-        start_ref[rows, :] = first - window_base - lane
+        turn = lax.rem(chunk, BLK // 128) * 128
+        begin = first - window_base - lane - (chunk * 128 - turn)
+        for j in range(span // 128):
+            ok = begin <= j * 128
+            if j * 128 >= tokens:
+                ok = ok & (lane + (j * 128 - tokens) <= sub + turn)
+            bias_ref[rows, j * 128 : j * 128 + 128] = jnp.where(ok, 0.0, NEG_FILL)
         return carry
 
     lax.fori_loop(0, tokens // 128, find_start, 0)
@@ -167,59 +173,69 @@
         gathers[0][d - 1].wait_recv()
         forwards[0][d].start()
 
-    lane32 = lax.broadcasted_iota(jnp.int32, (32, 128), 1)
-    sub32 = lax.broadcasted_iota(jnp.int32, (32, 128), 0)
-
     def heads_of(ref, rows):
         return jnp.concatenate([ref[rows, 0:HD], ref[rows, HD : 2 * HD]], axis=0)
 
     def middle(b):
         return tokens - b * BLK
 
-    def score(b, first, last):
-        rows, cols = slice(b * BLK, b * BLK + BLK), slice(b * BLK + first, b * BLK + last)
-        s_ref[b, :, first:last] = dot(heads_of(q_ref, rows), kv_ref[0, :, cols])
-
-    def masked(b, r, j, begin):
-        low, first = r % BLK, j * 128 - tokens
-        part = s_ref[b, r : r + 32, j * 128 : j * 128 + 128]
-        ok = begin <= b * BLK + j * 128
-        if first + 127 > low:
-            ok = ok & (lane32 + first <= sub32 + low)
-        return jnp.where(ok, part, NEG_FILL)
+    def scores(b, first, last):
+        def piece(col):
+            rows = slice(b * BLK, b * BLK + BLK)
+            cols = slice(b * BLK + col, b * BLK + col + BLK)
+            bias = bias_ref[rows, col : col + BLK]
+            part = dot(heads_of(q_ref, rows), kv_ref[0, :, cols])
+            s_ref[b, 0:BLK, col : col + BLK] = part[0:BLK] + bias
+            s_ref[b, BLK : 2 * BLK, col : col + BLK] = part[BLK : 2 * BLK] + bias
+
+        return [functools.partial(piece, col) for col in range(first, last, BLK)]
 
     def own_max(b):
-        for r in range(0, 2 * BLK, 32):
+        def piece(r):
             head, low = r // BLK, b * BLK + r % BLK
-            begin = start_ref[low : low + 32, :]
-            top = masked(b, r, middle(b) // 128, begin)
-            for j in range(middle(b) // 128 + 1, span // 128):
-                top = jnp.maximum(top, masked(b, r, j, begin))
+            first = middle(b) // 128
+            top = s_ref[b, r : r + 32, first * 128 : first * 128 + 128]
+            for j in range(first + 1, span // 128):
+                top = jnp.maximum(top, s_ref[b, r : r + 32, j * 128 : j * 128 + 128])
             max_ref[head, low : low + 32, :] = top
 
+        return [functools.partial(piece, r) for r in range(0, 2 * BLK, 32)]
+
     def row_max(b):
-        for r in range(0, 2 * BLK, 32):
+        def piece(r):
             head, low = r // BLK, b * BLK + r % BLK
-            begin = start_ref[low : low + 32, :]
             top = max_ref[head, low : low + 32, :]
             for j in range(middle(b) // 128):
-                top = jnp.maximum(top, masked(b, r, j, begin))
+                top = jnp.maximum(top, s_ref[b, r : r + 32, j * 128 : j * 128 + 128])
             top = jnp.max(top, axis=1, keepdims=True)
             max_ref[head, low : low + 32, :] = jnp.broadcast_to(top, (32, 128))
 
+        return [functools.partial(piece, r) for r in range(0, 2 * BLK, 32)]
+
     def probabilities(b):
-        for r in range(0, 2 * BLK, 32):
+        def piece(r):
             head, low = r // BLK, b * BLK + r % BLK
-            begin = start_ref[low : low + 32, :]
             top = max_ref[head, low : low + 32, :]
             total = jnp.zeros((32, 128), jnp.float32)
             for j in range(span // 128):
-                prob = jnp.exp2((masked(b, r, j, begin) - top) * factor)
+                part = s_ref[b, r : r + 32, j * 128 : j * 128 + 128]
+                prob = jnp.exp2((part - top) * factor)
                 total = total + prob
                 cols = slice(b * BLK + j * 128, b * BLK + j * 128 + 128)
                 p_ref[head, low : low + 32, cols] = prob.astype(jnp.bfloat16)
             inverse = 1.0 / jnp.sum(total, axis=1, keepdims=True)
             inv_ref[head, low : low + 32, :] = jnp.broadcast_to(inverse, (32, 128))
+
+        return [functools.partial(piece, r) for r in range(0, 2 * BLK, 32)]
+
+    def weave(*lists):
+        order = [
+            ((n + 0.5) / len(pieces_of), k, piece)
+            for k, pieces_of in enumerate(lists)
+            for n, piece in enumerate(pieces_of)
+        ]
+        for _, _, piece in sorted(order, key=lambda entry: entry[:2]):
+            piece()
 
     def scaled_turned(src_ref, dst_ref, b):
         rows = slice(b * BLK, b * BLK + BLK)
@@ -292,25 +308,24 @@
             result = result + rs_recv[i, d - 1].astype(jnp.float32)
         (dkt_ref, dvt_ref)[i][...] = result.astype(jnp.bfloat16)
 
-    score(0, middle(0), span)
+    weave(scores(0, middle(0), span))
     for b in range(blocks):
-        if b + 1 < blocks:
-            score(b + 1, middle(b + 1), span)
-        own_max(b)
+        ahead = scores(b + 1, middle(b + 1), span) if b + 1 < blocks else []
+        weave(ahead, own_max(b))
     for d in range(share):
         forwards[0][d].wait_recv()
 
-    score(0, 0, middle(0))
-    row_max(0)
-    score(1, 0, middle(1))
+    weave(scores(0, 0, middle(0)))
+    weave(scores(1, 0, middle(1)), row_max(0))
     for b in range(blocks):
+        matrix, vector = [], []
+        if b:
+            matrix.append(functools.partial(column_back, 1, b - 1))
         if b + 2 < blocks:
-            score(b + 2, 0, middle(b + 2))
+            matrix += scores(b + 2, 0, middle(b + 2))
         if b + 1 < blocks:
-            row_max(b + 1)
-        if b:
-            column_back(1, b - 1)
-        probabilities(b)
+            vector = row_max(b + 1)
+        weave(matrix, vector, probabilities(b))
         scaled_turned(do_ref, dot_ref, b)
         if b:
             backs[1][b - 1].start()
@@ -342,19 +357,13 @@
             delta = jnp.sum(grads * part.astype(jnp.float32), axis=1, keepdims=True)
             delta_ref[h, rows, :] = jnp.broadcast_to(delta, (BLK, 128))
 
-    for b in range(blocks):
-        outputs(b)
-        if b == 0:
-            for kc in range(blocks):
-                add_returned(1, kc, total_ref[1, :, kc * BLK : (kc + 1) * BLK])
-                if kc % 2:
-                    for c in scatters[1][kc // 2]:
-                        c.start()
-
-    def score_grads(b, kc):
+    def tile_change(b, kc):
         rows, cols = slice(b * BLK, b * BLK + BLK), slice(kc * BLK, kc * BLK + BLK)
-        change = dot(heads_of(do_ref, rows), kv_ref[1, :, cols])
-        for r in range(0, 2 * BLK, 64):
+        return dot(heads_of(do_ref, rows), kv_ref[1, :, cols])
+
+    def tile_scores(b, kc, change):
+        def piece(r):
+            cols = slice(kc * BLK, kc * BLK + BLK)
             head, low = r // BLK, r % BLK
             these = slice(b * BLK + low, b * BLK + low + 64)
             delta = delta_ref[head, these, :]
@@ -362,30 +371,74 @@
             held = p_ref[head, these, cols].astype(jnp.float32)
             p_ref[head, these, cols] = (held * (change[r : r + 64] - delta)).astype(jnp.bfloat16)
 
-    for b in rows_of(0):
-        score_grads(b, 0)
-    for kc in range(2 * blocks):
-        if kc + 1 < 2 * blocks:
-            for b in rows_of(kc + 1):
-                score_grads(b, kc + 1)
-        if kc < blocks:
-            column_back(0, kc)
-            backs[0][kc].start()
-        else:
-            add_returned(0, kc - blocks, column_sum(0, kc))
-            for c in scatters[0][kc - blocks]:
-                c.start()
-
-    k_ref[...] = kv_ref[0].T
-    finish(1)
-
-    for b in range(blocks):
+        return [functools.partial(piece, r) for r in range(0, 2 * BLK, 64)]
+
+    def query_grads(b):
         rows, window = slice(b * BLK, b * BLK + BLK), slice(b * BLK, b * BLK + span)
         dscore = jnp.concatenate([p_ref[0, rows, window], p_ref[1, rows, window]], axis=0)
         sums = dot(dscore, k_ref[window, :])
         for h in range(2):
             part = sums[h * BLK : h * BLK + BLK] * (inv_ref[h, rows, :] * scale)
             dq_ref[rows, h * HD : h * HD + HD] = part.astype(jnp.bfloat16)
+
+    outputs(0)
+    for kc in range(blocks):
+        add_returned(1, kc, total_ref[1, :, kc * BLK : (kc + 1) * BLK])
+        if kc % 2:
+            for c in scatters[1][kc // 2]:
+                c.start()
+
+    tiles = [(b, kc) for kc in range(2 * blocks) for b in rows_of(kc)]
+    change = tile_change(*tiles[0])
+    column = [None]
+    ready = []
+    for number, (b, kc) in enumerate(tiles):
+        following = [None]
+        matrix = []
+        if number + 1 < len(tiles):
+
+            def ahead(number=number, following=following):
+                following[0] = tile_change(*tiles[number + 1])
+
+            matrix.append(ahead)
+        if ready:
+            which = ready[0]
+
+            def total(which=which):
+                if which < blocks:
+                    column_back(0, which)
+                else:
+                    column[0] = column_sum(0, which)
+
+            matrix.append(total)
+            if which < blocks - 1:
+                matrix.append(functools.partial(outputs, which + 2)) if which + 2 < blocks else None
+        if number == 0:
+            matrix.append(functools.partial(outputs, 1))
+        weave(matrix, tile_scores(b, kc, change))
+        change = following[0]
+        if ready:
+            which = ready.pop()
+            if which < blocks:
+                backs[0][which].start()
+            else:
+                add_returned(0, which - blocks, column[0])
+                for c in scatters[0][which - blocks]:
+                    c.start()
+            if which == blocks - 1:
+                k_ref[...] = kv_ref[0].T
+            if which in (blocks, blocks + 1):
+                query_grads(which - blocks)
+        if b == rows_of(kc)[-1]:
+            ready.append(kc)
+    add_returned(0, blocks - 1, column_sum(0, 2 * blocks - 1))
+    for c in scatters[0][blocks - 1]:
+        c.start()
+
+    finish(1)
+
+    for b in range(2, blocks):
+        query_grads(b)
 
     finish(0)
 
@@ -428,7 +481,7 @@
             pltpu.VMEM((2, HD, 2 * tokens), bf16),
             pltpu.VMEM((2 * tokens, HD), bf16),
             pltpu.VMEM((2 * tokens, HD), bf16),
-            pltpu.VMEM((tokens, 128), jnp.int32),
+            pltpu.VMEM((tokens, tokens + BLK), f32),
             pltpu.VMEM((blocks, 2 * BLK, tokens + BLK), f32),
             pltpu.VMEM((2, tokens, 2 * tokens), bf16),
             pltpu.VMEM((2, tokens, 128), f32),

time: 43 us -> 43.1 us (level)
  no operation moved by 1% of the time
where the time goes in v5:
time: 43.1 us; the launch traced here: 42.9 us
  Pallas kernels  42.3 us (98%)
  between operations  0.64 us (1%)
    pallas_call x1, Pallas kernels, on_device(): pl.pallas_call(functools.partial(kernel, n_ctx, tokens, share), out_shape...  41.3 us
    pallas_call x1, Pallas kernels, on_device(): pl.pallas_call(hand_over, out_shape=[jax.ShapeDtypeStruct(shape, bf16) fo...  1.03 us

profile of v5, /device:TPU:1, one launch (start us, length us, event | category | flops | bytes accessed | tf_op | source)
XLA Modules:
  0.0 42.9 jit_solution(12503341277992697000)
XLA Ops:
  0.6 41.3 %shard_map.84 = (bf16[1024,256]{1,0:T(8,128)(2,1)S(1)}, bf16[1024,256]{1,0:T(8,128)(2,1)S(1)}, bf16[32,1024]{1,0:T(8,128)(2,1)S(1)}, bf16[32,1024]{1,0:T(8,128)(2,1)S(1)}) custom-call(s32[32]{0:T(128)} %doc_ref.1, bf16[1024,256]{1,0:T(8,128)(2,1)} %q_hbm.1, bf16[32,1024]{1,0:T(8,128)(2,1)} %bitcast.4, bf16[32,1024]{1,0:T(8,128)(2,1)} %bitcast.5, ...), custom_call_target="tpu_custom_call" | custom-call | flops 4026531840 | bytes 2097152 | tf_op jit(solution)/shard_map/pallas_call | solution.py:471
  41.9 1.0 %shard_map.85 = (bf16[1024,256]{1,0:T(8,128)(2,1)}, bf16[1024,256]{1,0:T(8,128)(2,1)}, bf16[32,1024]{1,0:T(8,128)(2,1)}, bf16[32,1024]{1,0:T(8,128)(2,1)}) custom-call(bf16[1024,256]{1,0:T(8,128)(2,1)S(1)} %get-tuple-element.12.refs_0_, bf16[1024,256]{1,0:T(8,128)(2,1)S(1)} %get-tuple-element.13.refs_1_, bf16[32,1024]{1,0:T(8,128)(2,1)S(1)} %get-tuple-element.14.refs_2_, ...), custom_call_target="tpu_custom_call" | custom-call | bytes 1048576 | tf_op jit(solution)/shard_map/pallas_call | solution.py:514

commit v6 on v5

--- a/solution.py
+++ b/solution.py
@@ -74,8 +74,17 @@
     before = pl.ds(0, tokens)
     kv_hbm = (kt_hbm, vt_hbm)
 
+    in_middle = lax.rem((place + 1) // 2, 2) == 1
+    at_an_end = jnp.logical_not(in_middle)
+    others = (
+        place,
+        place + 1 - 2 * lax.rem(place, 2),
+        place + 2 - 4 * (place // 2),
+        share - 1 - place,
+    )
+
     def other(d):
-        return lax.rem(place + d, share)
+        return others[d]
 
     def band_of(index):
         return pl.ds(pl.multiple_of(index * band, band), band)
@@ -115,11 +124,10 @@
         return copies
 
     def forward(i, d):
-        which = lax.rem(place - d + share, share)
-        src = kv_hbm[i] if d == 0 else kv_ref.at[i, band_of(which), own]
+        src = kv_hbm[i] if d == 0 else kv_ref.at[i, band_of(other(d)), own]
         return pltpu.make_async_remote_copy(
             src_ref=src,
-            dst_ref=kv_ref.at[i, band_of(which), before],
+            dst_ref=kv_ref.at[i, band_of(other(d)), before],
             send_sem=f_send.at[i, d],
             recv_sem=f_recv.at[i, d],
             device_id=(nxt, tp),
@@ -271,23 +279,61 @@
 
     pieces = ((1,) * blocks, (blocks // 2,) * 2)
 
-    def scatter(i, piece, d):
-        size = pieces[i][piece] * BLK
-        cols = pl.ds(sum(pieces[i][:piece]) * BLK, size)
+    def straight(i, piece):
+        return i == 0 and piece == len(pieces[0]) - 1
+
+    def columns_of(i, piece):
+        first = sum(pieces[i][:piece]) * BLK
+        return slice(first, first + pieces[i][piece] * BLK)
+
+    def scatter(i, piece, band, target, slot):
+        span_of = columns_of(i, piece)
+        cols = pl.ds(span_of.start, span_of.stop - span_of.start)
         return pltpu.make_async_remote_copy(
-            src_ref=rs_send.at[i, band_of(other(d)), cols],
-            dst_ref=rs_recv.at[i, d - 1, :, cols],
-            send_sem=r_send.at[i, piece, d - 1],
-            recv_sem=r_recv.at[i, piece, d - 1],
-            device_id=(ctx, base + other(d)),
+            src_ref=rs_send.at[i, band_of(other(band)), cols],
+            dst_ref=rs_recv.at[i, slot, :, cols],
+            send_sem=r_send.at[i, piece, slot],
+            recv_sem=r_recv.at[i, piece, slot],
+            device_id=(ctx, base + other(target)),
             device_id_type=MESH,
         )
 
     backs = [[back(i, kc) for kc in range(blocks)] for i in range(2)]
     scatters = [
-        [[scatter(i, piece, d) for d in range(1, share)] for piece in range(len(pieces[i]))]
+        [[scatter(i, piece, d, d, d - 1) for d in range(1, share)] for piece in range(len(pieces[i]))]
         for i in range(2)
     ]
+    relays = [
+        [scatter(i, piece, 3, 1, 3) for piece in range(len(pieces[i])) if not straight(i, piece)]
+        for i in range(2)
+    ]
+
+    def send_piece(i, piece):
+        first, second, third = scatters[i][piece]
+        if straight(i, piece):
+            second.start()
+            third.start()
+            first.start()
+            return
+
+        @pl.when(at_an_end)
+        def _():
+            relays[i][piece].start()
+            second.start()
+
+        pl.when(in_middle)(third.start)
+        first.start()
+
+    def add_on_the_way(i, piece):
+        cols = columns_of(i, piece)
+
+        @pl.when(in_middle)
+        def _():
+            relays[i][piece].wait_recv()
+            total = total_ref[i, band_of(other(2)), cols]
+            total = total + rs_recv[i, 3, :, cols].astype(jnp.float32)
+            rs_send[i, band_of(other(2)), cols] = total.astype(jnp.bfloat16)
+            scatters[i][piece][1].start()
 
     def column_back(i, kc):
         ret_send[i, :, kc * BLK : (kc + 1) * BLK] = column_sum(i, kc).astype(jnp.bfloat16)
@@ -300,11 +346,21 @@
         rs_send[i, :, cols] = total.astype(jnp.bfloat16)
 
     def finish(i):
-        for piece in scatters[i]:
-            for c in piece:
-                c.wait_recv()
+        for piece in range(len(pieces[i])):
+            cols = columns_of(i, piece)
+
+            def add_third(piece=piece, cols=cols):
+                scatters[i][piece][2].wait_recv()
+                total_ref[i, band_of(place), cols] += rs_recv[i, 2, :, cols].astype(jnp.float32)
+
+            if straight(i, piece):
+                add_third()
+            else:
+                pl.when(in_middle)(add_third)
+            scatters[i][piece][0].wait_recv()
+            scatters[i][piece][1].wait_recv()
         result = total_ref[i, band_of(place), :]
-        for d in range(1, share):
+        for d in range(1, share - 1):
             result = result + rs_recv[i, d - 1].astype(jnp.float32)
         (dkt_ref, dvt_ref)[i][...] = result.astype(jnp.bfloat16)
 
@@ -342,6 +398,10 @@
     for b in range(blocks):
         scaled_turned(q_ref, qt_ref, b)
     v_ref[own, :] = kv_ref[1, :, own].T
+    for kc in range(blocks):
+        add_returned(1, kc, total_ref[1, :, kc * BLK : (kc + 1) * BLK])
+        if kc % 2:
+            send_piece(1, kc // 2)
     for d in range(share):
         forwards[1][d].wait_recv()
     v_ref[before, :] = kv_ref[1, :, before].T
@@ -382,11 +442,6 @@
             dq_ref[rows, h * HD : h * HD + HD] = part.astype(jnp.bfloat16)
 
     outputs(0)
-    for kc in range(blocks):
-        add_returned(1, kc, total_ref[1, :, kc * BLK : (kc + 1) * BLK])
-        if kc % 2:
-            for c in scatters[1][kc // 2]:
-                c.start()
 
     tiles = [(b, kc) for kc in range(2 * blocks) for b in rows_of(kc)]
     change = tile_change(*tiles[0])
@@ -423,27 +478,43 @@
                 backs[0][which].start()
             else:
                 add_returned(0, which - blocks, column[0])
-                for c in scatters[0][which - blocks]:
-                    c.start()
+                send_piece(0, which - blocks)
             if which == blocks - 1:
                 k_ref[...] = kv_ref[0].T
+                for piece in range(len(pieces[1])):
+                    add_on_the_way(1, piece)
             if which in (blocks, blocks + 1):
                 query_grads(which - blocks)
         if b == rows_of(kc)[-1]:
             ready.append(kc)
     add_returned(0, blocks - 1, column_sum(0, 2 * blocks - 1))
-    for c in scatters[0][blocks - 1]:
-        c.start()
+    send_piece(0, blocks - 1)
+    for piece in range(blocks - 2):
+        add_on_the_way(0, piece)
+    query_grads(2)
+    add_on_the_way(0, blocks - 2)
+    query_grads(3)
 
     finish(1)
-
-    for b in range(2, blocks):
-        query_grads(b)
-
     finish(0)
 
+    always = gathers[1] + forwards[0] + forwards[1] + backs[0] + backs[1]
+    middle_only, end_only = [], relays[0] + relays[1]
     for i in range(2):
-        for c in (gathers[i] if i else []) + forwards[i] + backs[i] + sum(scatters[i], []):
+        for piece, (first, second, third) in enumerate(scatters[i]):
+            always += [first, second]
+            (always if straight(i, piece) else middle_only).append(third)
+    for c in always:
+        c.wait_send()
+
+    @pl.when(in_middle)
+    def _():
+        for c in middle_only:
+            c.wait_send()
+
+    @pl.when(at_an_end)
+    def _():
+        for c in end_only:
             c.wait_send()
 
 
@@ -491,7 +562,7 @@
             pltpu.VMEM((2, HD, tokens), bf16),
             pltpu.VMEM((2, HD, tokens), f32),
             pltpu.VMEM((2, HD, tokens), bf16),
-            pltpu.VMEM((2, share - 1, columns, tokens), bf16),
+            pltpu.VMEM((2, share, columns, tokens), bf16),
             dma((4,)),
             dma((2, share - 1)),
             dma((2, share - 1)),
@@ -499,8 +570,8 @@
             dma((2, share)),
             dma((2, blocks)),
             dma((2, blocks)),
-            dma((2, blocks, share - 1)),
-            dma((2, blocks, share - 1)),
+            dma((2, blocks, share)),
+            dma((2, blocks, share)),
         ],
         compiler_params=pltpu.CompilerParams(
             collective_id=0, has_side_effects=True, vmem_limit_bytes=60 * 1024 * 1024

time: 43.1 us -> 43 us (level)
  no operation moved by 1% of the time
where the time goes in v6:
time: 43 us; the launch traced here: 42.7 us
  Pallas kernels  42.1 us (98%)
  between operations  0.64 us (1%)
    pallas_call x1, Pallas kernels, on_device(): pl.pallas_call(functools.partial(kernel, n_ctx, tokens, share), out_shape...  41.1 us
    pallas_call x1, Pallas kernels, on_device(): pl.pallas_call(hand_over, out_shape=[jax.ShapeDtypeStruct(shape, bf16) fo...  1.03 us

profile of v6, /device:TPU:1, one launch (start us, length us, event | category | flops | bytes accessed | tf_op | source)
XLA Modules:
  0.0 42.7 jit_solution(17690774686187648686)
XLA Ops:
  0.6 41.1 %shard_map.84 = (bf16[1024,256]{1,0:T(8,128)(2,1)S(1)}, bf16[1024,256]{1,0:T(8,128)(2,1)S(1)}, bf16[32,1024]{1,0:T(8,128)(2,1)S(1)}, bf16[32,1024]{1,0:T(8,128)(2,1)S(1)}) custom-call(s32[32]{0:T(128)} %doc_ref.1, bf16[1024,256]{1,0:T(8,128)(2,1)} %q_hbm.1, bf16[32,1024]{1,0:T(8,128)(2,1)} %bitcast.4, bf16[32,1024]{1,0:T(8,128)(2,1)} %bitcast.5, ...), custom_call_target="tpu_custom_call" | custom-call | flops 4026531840 | bytes 2097152 | tf_op jit(solution)/shard_map/pallas_call | solution.py:542
  41.7 1.0 %shard_map.85 = (bf16[1024,256]{1,0:T(8,128)(2,1)}, bf16[1024,256]{1,0:T(8,128)(2,1)}, bf16[32,1024]{1,0:T(8,128)(2,1)}, bf16[32,1024]{1,0:T(8,128)(2,1)}) custom-call(bf16[1024,256]{1,0:T(8,128)(2,1)S(1)} %get-tuple-element.12.refs_0_, bf16[1024,256]{1,0:T(8,128)(2,1)S(1)} %get-tuple-element.13.refs_1_, bf16[32,1024]{1,0:T(8,128)(2,1)S(1)} %get-tuple-element.14.refs_2_, ...), custom_call_target="tpu_custom_call" | custom-call | bytes 1048576 | tf_op jit(solution)/shard_map/pallas_call | solution.py:585

commit v7 on v5

--- a/solution.py
+++ b/solution.py
@@ -16,6 +16,10 @@
 
 def dot(a, b):
     return jnp.dot(a, b, preferred_element_type=jnp.float32)
+
+
+def dot_rows(a, b):
+    return lax.dot_general(a, b, (((1,), (1,)), ((), ())), preferred_element_type=jnp.float32)
 
 
 def kernel(
@@ -36,14 +40,11 @@
     qt_ref,
     dot_ref,
     kv_ref,
-    k_ref,
-    v_ref,
     bias_ref,
     s_ref,
     p_ref,
     delta_ref,
     max_ref,
-    inv_ref,
     ret_send,
     ret_recv,
     total_ref,
@@ -161,7 +162,9 @@
 
     lax.fori_loop(0, tokens // 128, find_start, 0)
     load_q.wait()
+    qt_ref[...] = q_ref[...].T
     load_do.wait()
+    dot_ref[...] = do_ref[...].T
 
     for c in gathers[0]:
         c.wait_send()
@@ -215,18 +218,19 @@
     def probabilities(b):
         def piece(r):
             head, low = r // BLK, b * BLK + r % BLK
-            top = max_ref[head, low : low + 32, :]
-            total = jnp.zeros((32, 128), jnp.float32)
+            top = max_ref[head, low : low + 16, :]
+            total = jnp.zeros((16, 128), jnp.float32)
+            probs = []
             for j in range(span // 128):
-                part = s_ref[b, r : r + 32, j * 128 : j * 128 + 128]
-                prob = jnp.exp2((part - top) * factor)
-                total = total + prob
+                part = s_ref[b, r : r + 16, j * 128 : j * 128 + 128]
+                probs.append(jnp.exp2((part - top) * factor))
+                total = total + probs[-1]
+            inverse = 1.0 / jnp.sum(total, axis=1, keepdims=True)
+            for j, prob in enumerate(probs):
                 cols = slice(b * BLK + j * 128, b * BLK + j * 128 + 128)
-                p_ref[head, low : low + 32, cols] = prob.astype(jnp.bfloat16)
-            inverse = 1.0 / jnp.sum(total, axis=1, keepdims=True)
-            inv_ref[head, low : low + 32, :] = jnp.broadcast_to(inverse, (32, 128))
-
-        return [functools.partial(piece, r) for r in range(0, 2 * BLK, 32)]
+                p_ref[head, low : low + 16, cols] = (prob * inverse).astype(jnp.bfloat16)
+
+        return [functools.partial(piece, r) for r in range(0, 2 * BLK, 16)]
 
     def weave(*lists):
         order = [
@@ -236,13 +240,6 @@
         ]
         for _, _, piece in sorted(order, key=lambda entry: entry[:2]):
             piece()
-
-    def scaled_turned(src_ref, dst_ref, b):
-        rows = slice(b * BLK, b * BLK + BLK)
-        for h in range(2):
-            cols = slice(h * HD, h * HD + HD)
-            part = src_ref[rows, cols].astype(jnp.float32) * inv_ref[h, rows, :]
-            dst_ref[cols, rows] = part.astype(jnp.bfloat16).T
 
     left = (qt_ref, dot_ref)
     weights = (scale, 1.0)
@@ -326,7 +323,6 @@
         if b + 1 < blocks:
             vector = row_max(b + 1)
         weave(matrix, vector, probabilities(b))
-        scaled_turned(do_ref, dot_ref, b)
         if b:
             backs[1][b - 1].start()
         if b == 2:
@@ -339,19 +335,20 @@
     backs[1][blocks - 1].start()
     for kc in range(blocks):
         total_ref[1, :, kc * BLK : (kc + 1) * BLK] = column_sum(1, kc + blocks)
-    for b in range(blocks):
-        scaled_turned(q_ref, qt_ref, b)
-    v_ref[own, :] = kv_ref[1, :, own].T
+    for kc in range(blocks):
+        add_returned(1, kc, total_ref[1, :, kc * BLK : (kc + 1) * BLK])
+        if kc % 2:
+            for c in scatters[1][kc // 2]:
+                c.start()
     for d in range(share):
         forwards[1][d].wait_recv()
-    v_ref[before, :] = kv_ref[1, :, before].T
 
     def outputs(b):
         rows, window = slice(b * BLK, b * BLK + BLK), slice(b * BLK, b * BLK + span)
         prob = jnp.concatenate([p_ref[0, rows, window], p_ref[1, rows, window]], axis=0)
-        sums = dot(prob, v_ref[window, :])
+        sums = dot_rows(prob, kv_ref[1, :, window])
         for h in range(2):
-            part = (sums[h * BLK : h * BLK + BLK] * inv_ref[h, rows, :]).astype(jnp.bfloat16)
+            part = sums[h * BLK : h * BLK + BLK].astype(jnp.bfloat16)
             out_ref[rows, h * HD : h * HD + HD] = part
             grads = do_ref[rows, h * HD : h * HD + HD].astype(jnp.float32)
             delta = jnp.sum(grads * part.astype(jnp.float32), axis=1, keepdims=True)
@@ -376,17 +373,12 @@
     def query_grads(b):
         rows, window = slice(b * BLK, b * BLK + BLK), slice(b * BLK, b * BLK + span)
         dscore = jnp.concatenate([p_ref[0, rows, window], p_ref[1, rows, window]], axis=0)
-        sums = dot(dscore, k_ref[window, :])
+        sums = dot_rows(dscore, kv_ref[0, :, window])
         for h in range(2):
-            part = sums[h * BLK : h * BLK + BLK] * (inv_ref[h, rows, :] * scale)
+            part = sums[h * BLK : h * BLK + BLK] * scale
             dq_ref[rows, h * HD : h * HD + HD] = part.astype(jnp.bfloat16)
 
     outputs(0)
-    for kc in range(blocks):
-        add_returned(1, kc, total_ref[1, :, kc * BLK : (kc + 1) * BLK])
-        if kc % 2:
-            for c in scatters[1][kc // 2]:
-                c.start()
 
     tiles = [(b, kc) for kc in range(2 * blocks) for b in rows_of(kc)]
     change = tile_change(*tiles[0])
@@ -425,8 +417,6 @@
                 add_returned(0, which - blocks, column[0])
                 for c in scatters[0][which - blocks]:
                     c.start()
-            if which == blocks - 1:
-                k_ref[...] = kv_ref[0].T
             if which in (blocks, blocks + 1):
                 query_grads(which - blocks)
         if b == rows_of(kc)[-1]:
@@ -479,12 +469,9 @@
             pltpu.VMEM((width, tokens), bf16),
             pltpu.VMEM((width, tokens), bf16),
             pltpu.VMEM((2, HD, 2 * tokens), bf16),
-            pltpu.VMEM((2 * tokens, HD), bf16),
-            pltpu.VMEM((2 * tokens, HD), bf16),
             pltpu.VMEM((tokens, tokens + BLK), f32),
             pltpu.VMEM((blocks, 2 * BLK, tokens + BLK), f32),
             pltpu.VMEM((2, tokens, 2 * tokens), bf16),
-            pltpu.VMEM((2, tokens, 128), f32),
             pltpu.VMEM((2, tokens, 128), f32),
             pltpu.VMEM((2, tokens, 128), f32),
             pltpu.VMEM((2, HD, tokens), bf16),

time: 43.1 us -> 42.9 us (level)
  no operation moved by 1% of the time
where the time goes in v7:
time: 42.9 us; the launch traced here: 42.7 us
  Pallas kernels  42.1 us (98%)
  between operations  0.64 us (1%)
    pallas_call x1, Pallas kernels, on_device(): pl.pallas_call(functools.partial(kernel, n_ctx, tokens, share), out_shape...  41.1 us
    pallas_call x1, Pallas kernels, on_device(): pl.pallas_call(hand_over, out_shape=[jax.ShapeDtypeStruct(shape, bf16) fo...  1.03 us

profile of v7, /device:TPU:1, one launch (start us, length us, event | category | flops | bytes accessed | tf_op | source)
XLA Modules:
  0.0 42.7 jit_solution(9100821925752319330)
XLA Ops:
  0.6 41.1 %shard_map.84 = (bf16[1024,256]{1,0:T(8,128)(2,1)S(1)}, bf16[1024,256]{1,0:T(8,128)(2,1)S(1)}, bf16[32,1024]{1,0:T(8,128)(2,1)S(1)}, bf16[32,1024]{1,0:T(8,128)(2,1)S(1)}) custom-call(s32[32]{0:T(128)} %doc_ref.1, bf16[1024,256]{1,0:T(8,128)(2,1)} %q_hbm.1, bf16[32,1024]{1,0:T(8,128)(2,1)} %bitcast.4, bf16[32,1024]{1,0:T(8,128)(2,1)} %bitcast.5, ...), custom_call_target="tpu_custom_call" | custom-call | flops 4026531840 | bytes 2097152 | tf_op jit(solution)/shard_map/pallas_call | solution.py:461
  41.7 1.0 %shard_map.85 = (bf16[1024,256]{1,0:T(8,128)(2,1)}, bf16[1024,256]{1,0:T(8,128)(2,1)}, bf16[32,1024]{1,0:T(8,128)(2,1)}, bf16[32,1024]{1,0:T(8,128)(2,1)}) custom-call(bf16[1024,256]{1,0:T(8,128)(2,1)S(1)} %get-tuple-element.12.refs_0_, bf16[1024,256]{1,0:T(8,128)(2,1)S(1)} %get-tuple-element.13.refs_1_, bf16[32,1024]{1,0:T(8,128)(2,1)S(1)} %get-tuple-element.14.refs_2_, ...), custom_call_target="tpu_custom_call" | custom-call | bytes 1048576 | tf_op jit(solution)/shard_map/pallas_call | solution.py:501
